TPU v7x, 128 devices: a whole 4x4x4 slice. The times are simulated.
128 devices in a mesh: prow: 16 (over x, y), pcol: 8 (over z, core).
Axes of the slice: x: 4, y: 4, z: 4, core: 2. Of those that a mesh axis runs over, the one named last changes fastest.
Arguments:
- matrix: float32 [16384, 16384], P('prow', 'pcol'), may hold values from -17 to 17
- pivots: int32 [128], replicated, may hold values from 0 to 16383, as said below
Outputs:
- updated: float32 [16384, 16384], P('prow', 'pcol')
Inputs may be any that keep to these rules, and one draw needn't show every extreme that they name: `pivots`: entry j lies between j and 16383; one entry equals 16383.
All inputs are finite; a program needn't handle non-finite values.
Results may differ from a plain program's by a relative error of at most 0.000075.
Values sent between devices are 32-bit elements; how exact they have to be, the bound alone decides.
A program may use at most 64 MiB of HBM per device.

v0:
```python
import jax
import jax.numpy as jnp
from jax import lax
from jax.sharding import PartitionSpec as P


def broadcast(value, axis, source):
    kept = jnp.where(lax.axis_index(axis) == source, value, 0).astype(value.dtype)
    return lax.psum(kept, axis)


def unit_lower(block, width):
    return jnp.tril(block, -1) + jnp.eye(width, dtype=jnp.float32)


def compose_all(perms):
    while perms.shape[0] > 1:
        earlier = perms[0::2]
        later = perms[1::2]
        perms = jnp.take_along_axis(earlier, later, axis=1)
    return perms[0]


def local(matrix, pivots):
    rows_dev, cols_dev = matrix.shape
    width = pivots.shape[0]
    row_rank = lax.axis_index("prow")
    col_rank = lax.axis_index("pcol")
    row_start = row_rank * rows_dev
    col_start = col_rank * cols_dev
    places = jnp.concatenate([jnp.arange(width, dtype=jnp.int32), pivots])
    slots = places.shape[0]
    slot_ids = jnp.arange(slots, dtype=jnp.int32)
    same = places[:, None] == places[None, :]
    canonical = jnp.min(jnp.where(same, slot_ids[None, :], slots), axis=1)
    steps = jnp.arange(width, dtype=jnp.int32)
    pivot_slot = canonical[width:]
    at_step = canonical[None, :] == steps[:, None]
    at_pivot = canonical[None, :] == pivot_slot[:, None]
    swaps = jnp.where(
        at_step, pivot_slot[:, None], jnp.where(at_pivot, steps[:, None], canonical[None, :])
    )
    final_slot = compose_all(swaps)
    anchor = places[final_slot]
    sources = anchor - row_start
    owned_rows = (sources >= 0) & (sources < rows_dev)
    picked = jnp.where(owned_rows[:, None], matrix[jnp.clip(sources, 0, rows_dev - 1)], 0.0)
    fetched = lax.psum(picked, "prow")
    targets = places - row_start
    inside = (targets >= 0) & (targets < rows_dev)
    swapped = matrix.at[jnp.where(inside, targets, rows_dev)].set(fetched, mode="drop")
    top_rows = fetched[:width]
    panel = broadcast(matrix[:, :width], "pcol", 0)
    global_rows = row_start + jnp.arange(rows_dev, dtype=jnp.int32)
    lower_part = jnp.where(global_rows[:, None] >= width, panel, 0.0)
    diag_part = unit_lower(panel[:width], width)
    solved = jax.scipy.linalg.solve_triangular(diag_part, top_rows, lower=True, unit_diagonal=True)
    upper_rows = broadcast(solved, "prow", 0)
    update = swapped - jnp.dot(
        lower_part, upper_rows, precision=lax.Precision.HIGHEST, preferred_element_type=jnp.float32
    )
    head_rows = jnp.where(row_rank == 0, upper_rows, update[:width])
    result = jnp.concatenate([head_rows, update[width:]], axis=0)
    global_cols = col_start + jnp.arange(cols_dev, dtype=jnp.int32)
    return jnp.where(global_cols[None, :] >= width, result, matrix)


def solution(mesh):
    placed = (P("prow", "pcol"), P())
    return jax.shard_map(
        local, mesh=mesh, in_specs=placed, out_specs=P("prow", "pcol"), check_vma=False
    )
```

profile of v0, /device:TPU:0, one launch (start us, length us, event | category | flops | bytes accessed | tf_op | source)
XLA Modules:
  0.0 482.5 jit_solution(1670996911277213036)
XLA Ops:
  6.5 0.0 all-reduce.4.cloned.1.call-start
  6.5 1.9 slice_select_fusion.1
  8.4 0.0 all-reduce.4.cloned.1.call-update
  8.4 0.0 all-reduce.6.cloned.1.call-start
  8.5 0.7 pad_add_fusion
  9.2 0.2 select_reduce_fusion
  9.4 0.1 select_select_fusion
  9.6 129.5 %gather_fusion.3 = s32[16384]{0:T(1024)S(1)} fusion(s32[64,256]{1,0:T(8,128)S(1)} %slice.71, s32[16384]{0:T(1024)S(1)} %bitcast.64), kind=kCustom, calls=%fused_computation.3 | custom fusion | bytes 262144 | tf_op jit(solution)/shard_map/jit(take_along_axis)/gather | solution.py:20
  139.2 65.0 %gather_fusion.4 = s32[8192]{0:T(1024)S(1)} fusion(s32[32,256]{1,0:T(8,128)S(1)} %slice.73, s32[8192]{0:T(1024)S(1)} %bitcast.66), kind=kCustom, calls=%fused_computation.4 | custom fusion | bytes 131072 | tf_op jit(solution)/shard_map/jit(take_along_axis)/gather | solution.py:20
  204.3 32.8 %gather_fusion.5 = s32[4096]{0:T(1024)S(1)} fusion(s32[16,256]{1,0:T(8,128)S(1)} %slice.75, s32[4096]{0:T(1024)S(1)} %bitcast.67), kind=kCustom, calls=%fused_computation.5 | custom fusion | bytes 65536 | tf_op jit(solution)/shard_map/jit(take_along_axis)/gather | solution.py:20
  237.2 13.0 %gather_fusion.6 = s32[2048]{0:T(1024)S(1)} fusion(s32[8,256]{1,0:T(8,128)S(1)} %slice.77, s32[2048]{0:T(1024)S(1)} %bitcast.68), kind=kCustom, calls=%fused_computation.6 | custom fusion | bytes 32768 | tf_op jit(solution)/shard_map/jit(take_along_axis)/gather | solution.py:20
  250.3 9.1 %gather_fusion.7 = s32[1024]{0:T(1024)S(1)} fusion(s32[4,256]{1,0:T(4,128)S(1)} %slice.79, s32[1024]{0:T(1024)S(1)} %bitcast.69), kind=kCustom, calls=%fused_computation.7 | custom fusion | bytes 16384 | tf_op jit(solution)/shard_map/jit(take_along_axis)/gather | solution.py:20
  259.5 4.8 %gather_fusion.8 = s32[512]{0:T(512)S(1)} fusion(s32[2,256]{1,0:T(2,128)S(1)} %slice.81, s32[512]{0:T(512)S(1)} %bitcast.70), kind=kCustom, calls=%fused_computation.8 | custom fusion | bytes 8192 | tf_op jit(solution)/shard_map/jit(take_along_axis)/gather | solution.py:20
  264.4 1.9 gather_fusion
  266.4 1.9 gather_fusion.1
  268.4 5.8 %gather_fusion.2 = f32[256,2048]{1,0:T(8,128)S(1)} fusion(f32[1024,2048]{1,0:T(8,128)} %param.2, s32[1024]{0:T(1024)S(1)} %pad_clamp_fusion), kind=kCustom, calls=%fused_computation.2 | custom fusion | bytes 4195328 | tf_op jit(solution)/shard_map/gather | solution.py:47
  274.2 1.5 broadcast_select_fusion
  275.7 0.0 all-reduce.6.cloned.1.call-update
  275.8 0.2 all-reduce.8.cloned.1.call-start
  276.0 0.0 all-reduce.4.cloned.1.call-done
  276.0 0.9 fusion.7
  277.0 9.8 %custom-call.4 = f32[1,128,128]{1,2,0:T(8,128)S(1)} custom-call(f32[1,128,128]{2,1,0:T(8,128)S(1)} %fusion.7), custom_call_target="InvertDiagBlocksLowerTriangular" | custom-call | tf_op jit(solution)/shard_map/jit(_solve_triangular)/triangular_solve | solution.py:57
  286.8 81.8 %all-reduce.6.cloned.1.call-done = f32[256,2048]{1,0:T(8,128)} async-done(((f32[256,2048]{1,0:T(8,128)}), f32[256,2048]{1,0:T(8,128)}) %all-reduce.6.cloned.1.call-update) | async-done | bytes 2097168 | tf_op jit(solution)/shard_map/psum | solution.py:48
  368.6 3.2 convolution_select_fusion
  371.8 0.0 all-reduce.8.cloned.1.call-update
  371.9 0.0 copy-start.3
  371.9 0.0 copy-start
  371.9 8.0 %copy.10 = f32[1024,2048]{1,0:T(8,128)} copy(f32[1024,2048]{1,0:T(8,128)} %param.2) | data formatting | bytes 16777216
  379.9 0.0 copy-done.3
  380.0 0.0 copy-done
  380.0 0.0 copy-start.2
  380.0 8.6 %scatter_fusion = f32[1024,2048]{1,0:T(8,128)} fusion(f32[1024,2048]{1,0:T(8,128)} %copy.10, s32[256]{0:T(256)S(1)} %bitcast.72, f32[256,2048]{1,0:T(8,128)S(1)} %copy-done), kind=kCustom, calls=%fused_computation.9 | custom fusion | bytes 6292480 | tf_op jit(solution)/shard_map/scatter | solution.py:51
  388.6 69.7 %all-reduce.8.cloned.1.call-done = f32[128,2048]{1,0:T(8,128)} async-done(((f32[128,2048]{1,0:T(8,128)}), f32[128,2048]{1,0:T(8,128)}) %all-reduce.8.cloned.1.call-update) | async-done | bytes 1048592 | tf_op jit(solution)/shard_map/psum | solution.py:9
  458.3 0.0 copy-done.2
  458.3 9.3 %convolution_subtract_fusion = f32[1024,2048]{1,0:T(8,128)S(1)} fusion(f32[1024,2048]{1,0:T(8,128)} %scatter_fusion, f32[128,2048]{1,0:T(8,128)} %all-reduce.8.cloned.1.call-done, f32[1024,128]{1,0:T(8,128)S(1)} %copy-done.2, pred[1024]{0:T(1024)(128)(4,1)S(1)} %add_compare_fusion.1), kind=kOutput, calls=%fused_computation.11 | convolution fusion | flops 3223453696 | bytes 18351104 | tf_op jit(solution)/shard_map/dot_general | solution.py:59
  467.6 0.0 copy-start.1
  467.6 0.9 slice.108
  468.6 0.3 copy-done.1
  468.8 0.1 slice_select_fusion
  469.0 7.0 %maximum_select_fusion = f32[1024,2048]{1,0:T(8,128)} fusion(f32[1024,2048]{1,0:T(8,128)} %param.2, f32[896,2048]{1,0:T(8,128)S(1)} %slice.108, f32[128,2048]{1,0:T(8,128)S(1)} %slice_select_fusion, pred[2048]{0:T(1024)(128)(4,1)S(1)} %add_compare_fusion), kind=kLoop, calls=%fused_computation.10 | loop fusion | flops 4194304 | bytes 25167872 | tf_op jit(solution)/shard_map/jit(_where)/select_n | solution.py:65
  (51 shorter events, 0.6 us)
Async XLA Ops:
  6.5 269.5 %all-reduce.4.cloned.1.call-start = ((), (), s32[]{:S(2)}) async-start(), calls=%async_computation | async-start | bytes 1048576 | tf_op jit(solution)/shard_map/psum | solution.py:9
  8.4 360.1 %all-reduce.6.cloned.1.call-start = ((), (), s32[]{:S(2)}) async-start(), calls=%async_computation.1 | async-start | bytes 4194304 | tf_op jit(solution)/shard_map/psum | solution.py:48
  275.8 182.5 %all-reduce.8.cloned.1.call-start = ((), (), s32[]{:S(2)}) async-start(), calls=%async_computation.2 | async-start | bytes 2097152 | tf_op jit(solution)/shard_map/psum | solution.py:9
  371.9 8.1 %copy-start.3 = (s32[128]{0:T(128)S(1)}, s32[128]{0:T(128)}, u32[]{:S(2)}) copy-start(s32[128]{0:T(128)} %param.3) | copy-start | bytes 1540
  371.9 8.1 %copy-start = (f32[256,2048]{1,0:T(8,128)S(1)}, f32[256,2048]{1,0:T(8,128)}, u32[]{:S(2)}) copy-start(f32[256,2048]{1,0:T(8,128)} %all-reduce.6.cloned.1.call-done) | copy-start | bytes 6291460
  380.0 78.3 %copy-start.2 = (f32[1024,128]{1,0:T(8,128)S(1)}, f32[1024,128]{1,0:T(8,128)}, u32[]{:S(2)}) copy-start(f32[1024,128]{1,0:T(8,128)} %all-reduce.4.cloned.1.call-done) | copy-start | bytes 1572868
  467.6 1.2 copy-start.1
Sparse Core Ops, SparseCore 0:
  9.7 63.3 all-reduce.3
  275.9 92.6 all-reduce.5
  372.0 86.2 all-reduce.7
where the time goes:
time: 483 us; the launch traced here: 482 us
  local copies, waits for them, and re-layouts  282 us (58%)
  waiting for transfers between devices  152 us (31%)
  other arithmetic  22.4 us (5%)
  between operations  13.6 us (3%)
  matrix products  12.6 us (3%)
    gather x13, local copies, waits for them, and re-layouts, compose_all(): perms = jnp.take_along_axis(earlier, later, axis=1)  256 us
    psum x1, waiting for transfers between devices, local(): fetched = lax.psum(picked, 'prow')  81.8 us
    psum x2, waiting for transfers between devices, broadcast(): return lax.psum(kept, axis)  69.7 us
    another operation x3, other arithmetic, local(): jax.scipy.linalg.solve_triangular(diag_part, top_rows, lower=True, unit_d...  10.7 us
  transfers between devices with their start and end apart: 3, of which 2 were waited for; matrix products, arithmetic and copies ran while one was open for 61% of the time, Pallas kernels for 0%

commit v1 on v0

v1 whole, which is shorter than its diff:
```python
import functools

import jax
import jax.numpy as jnp
from jax import lax
from jax.experimental import pallas as pl
from jax.experimental.pallas import tpu as pltpu
from jax.sharding import PartitionSpec as P

NB = 128
PROWS = 16
SIDE = 4
FEW = 24
VMEM_BYTES = 60 * 1024 * 1024
HIGHEST = lax.Precision.HIGHEST


def plan_kernel(
    pivots, matrix, picks, owner, slot, leaving, place, info, arrangement, count, sems
):
    rows_dev = matrix.shape[0]
    me = lax.axis_index("prow")

    def start_top(j, carry):
        arrangement[j] = j
        return carry

    def start_pivot(j, carry):
        p = pivots[j]
        arrangement[p] = p
        return carry

    def start_count(r, carry):
        count[r] = 0
        return carry

    lax.fori_loop(0, NB, start_top, 0, unroll=8)
    lax.fori_loop(0, NB, start_pivot, 0, unroll=8)
    lax.fori_loop(0, PROWS, start_count, 0, unroll=8)

    def row_copy(source, s):
        return pltpu.make_async_copy(
            matrix.at[pl.ds(source, 1), :], picks.at[pl.ds(s, 1), :], sems.at[s]
        )

    def interchange(j, carry):
        p = pivots[j]
        first = arrangement[j]
        second = arrangement[p]
        arrangement[j] = second
        arrangement[p] = first
        r = second // rows_dev
        s = count[r]
        count[r] = s + 1
        owner[j] = r
        slot[j] = s

        @pl.when(r == me)
        def _():
            source = second - r * rows_dev
            row_copy(source, s).start()
            place[s] = jnp.where(second >= NB, source, -1)

        return carry

    lax.fori_loop(0, NB, interchange, 0, unroll=4)

    def leave(j, carry):
        leaving[owner[j] * NB + slot[j]] = arrangement[arrangement[j]]
        return carry

    lax.fori_loop(0, NB, leave, 0, unroll=4)

    def most(r, carry):
        return jnp.maximum(carry, count[r])

    info[0] = count[me]
    info[1] = lax.fori_loop(0, PROWS, most, 0, unroll=8)

    def finish(s, carry):
        row_copy(0, s).wait()
        return carry

    lax.fori_loop(0, count[me], finish, 0)


def invert_unit_lower(block):
    rows = lax.broadcasted_iota(jnp.int32, (NB, NB), 0)
    cols = lax.broadcasted_iota(jnp.int32, (NB, NB), 1)
    eye = jnp.where(rows == cols, 1.0, 0.0).astype(jnp.float32)
    dot = functools.partial(jnp.dot, precision=HIGHEST, preferred_element_type=jnp.float32)
    inverse = eye
    size = 1
    while size < NB:
        corner = (rows // size == cols // size + 1) & (rows // (2 * size) == cols // (2 * size))
        part = jnp.where(corner, block, 0.0)
        if size == 1:
            inverse = eye - part
        else:
            inverse = inverse - dot(dot(inverse, part), inverse)
        size *= 2
    return inverse


def exchange_kernel(
    slots,
    owner, slot, leaving, matrix, picks,
    gathered, panel, inverse, returned,
    received, ordered, top, top_a, top_b, back, corner,
    row_send, row_recv, ret_send, ret_recv, ring_send, ring_recv,
    top_send, top_recv, panel_send, panel_recv, inv_send, inv_recv, own_sem,
):
    half, quarter = NB // 2, NB // 4
    rows_dev = matrix.shape[0]
    me = lax.axis_index("prow")
    col = lax.axis_index("pcol")
    x, y = me // SIDE, me % SIDE
    z, core = col // 2, col % 2
    sent = []

    def block(q):
        return pl.ds(pl.multiple_of(q * NB, NB), NB)

    def remote(src, dst, send_sem, recv_sem, device):
        return pltpu.make_async_remote_copy(
            src_ref=src, dst_ref=dst, send_sem=send_sem, recv_sem=recv_sem, device_id=device
        )

    z_up, z_down = ((z + 1) % 4) * 2 + core, ((z + 3) % 4) * 2 + core
    other = z * 2 + 1 - core
    barrier = pltpu.get_barrier_semaphore()
    for d in range(1, PROWS):
        pl.semaphore_signal(barrier, inc=1, device_id={"prow": (me + d) % PROWS})
    for c in (z_up, z_down, other):
        pl.semaphore_signal(barrier, inc=1, device_id={"pcol": c})

    own_rows = pltpu.make_async_copy(
        picks.at[pl.ds(0, slots), block(me)],
        received.at[pl.ds(pl.multiple_of(me * slots, 8), slots)],
        own_sem.at[0],
    )
    own_rows.start()
    pl.semaphore_wait(barrier, PROWS - 1 + 3)

    def row_copy(d):
        peer = (me + d) % PROWS
        return remote(
            picks.at[pl.ds(0, slots), block(peer)],
            received.at[pl.ds(pl.multiple_of(me * slots, 8), slots)],
            row_send.at[d], row_recv.at[d], {"prow": peer},
        )

    def row_start(d, carry):
        row_copy(d).start()
        return carry

    def row_wait(d, carry):
        row_copy(d).wait_recv()
        return carry

    def row_sent(d, carry):
        row_copy(d).wait_send()
        return carry

    lax.fori_loop(1, PROWS, row_start, 0)

    def top_x(d):
        return remote(
            matrix.at[pl.ds(0, half), pl.ds(d * SIDE * NB, SIDE * NB)], top_a,
            top_send.at[d], top_recv.at[0], {"prow": d * SIDE},
        )

    def top_y(d, k):
        return remote(
            matrix.at[pl.ds(half, half), pl.ds((k * SIDE + d) * NB, NB)],
            top_b.at[:, pl.ds(k * NB, NB)],
            top_send.at[4 + 4 * d + k], top_recv.at[1 + k], {"prow": d},
        )

    top_own = [
        pltpu.make_async_copy(
            matrix.at[pl.ds(0, half), pl.ds(0, SIDE * NB)], top_a, own_sem.at[1]
        )
    ] + [
        pltpu.make_async_copy(
            matrix.at[pl.ds(half, half), pl.ds(k * SIDE * NB, NB)],
            top_b.at[:, pl.ds(k * NB, NB)], own_sem.at[2 + k],
        )
        for k in range(SIDE)
    ]
    diagonal = pltpu.make_async_copy(matrix.at[pl.ds(0, NB), pl.ds(0, NB)], corner, own_sem.at[6])

    @pl.when(me == 0)
    def _():
        for d in (1, 3, 2):
            top_x(d).start()
            for k in range(SIDE):
                top_y(d, k).start()
        for c in top_own:
            c.start()

    halves = [pl.ds(0, rows_dev // 2), pl.ds(rows_dev // 2, rows_dev // 2)]
    first_panel = matrix.at[:, pl.ds(0, NB)]

    def panel_first(h, k, to):
        return remote(
            first_panel.at[halves[h]], panel.at[halves[h]],
            panel_send.at[k], panel_recv.at[h], {"pcol": to},
        )

    def panel_next(h, k, to):
        return remote(
            panel.at[halves[h]], panel.at[halves[h]],
            panel_send.at[k], panel_recv.at[h], {"pcol": to},
        )

    panel_own = pltpu.make_async_copy(first_panel, panel, own_sem.at[7])

    @pl.when(col == 0)
    def _():
        panel_first(0, 0, z_up).start()
        panel_first(1, 1, z_down).start()
        panel_first(1, 2, z_up).start()
        panel_first(0, 3, z_down).start()
        panel_first(0, 4, other).start()
        panel_first(1, 5, other).start()
        panel_own.start()

    @pl.when((me == 0) & (col == 0))
    def _():
        diagonal.start()
        diagonal.wait()
        inverse[...] = invert_unit_lower(corner[...])

    own_rows.wait()
    lax.fori_loop(1, PROWS, row_wait, 0)

    def order(j, carry):
        ordered[pl.ds(j, 1), :] = received[pl.ds(owner[j] * slots + slot[j], 1), :]
        return carry

    lax.fori_loop(0, NB, order, 0, unroll=8)
    gathered[:, block(me)] = ordered[...]

    def at(xx, yy):
        return ((xx + 2 * SIDE) % SIDE) * SIDE + (yy + 2 * SIDE) % SIDE

    class Ring:
        def __init__(self, o):
            self.o = o
            self.row0 = o * half

        def where(self, along, across):
            return at(x + along, y + across) if self.o == 0 else at(x + across, y + along)

        def device(self, along, across):
            return {"prow": self.where(along, across)}

        def copy(self, q, part, sem, device):
            start, size = ((0, half), (0, quarter), (quarter, quarter))[part]
            ref = gathered.at[pl.ds(self.row0 + start, size), block(q)]
            return remote(ref, ref, ring_send.at[self.o, sem], ring_recv.at[self.o, sem], device)

        def send(self, q, part, sem, device):
            c = self.copy(q, part, sem, device)
            c.start()
            sent.append(c)

        def wait(self, q, part, sem):
            self.copy(q, part, sem, self.device(0, 1)).wait_recv()

    rings = (Ring(0), Ring(1))
    steps = (0, -1, 1, 2)

    def first_own(ring):
        q = ring.where(0, 0)
        ring.send(q, 0, 0, ring.device(1, 0))
        ring.send(q, 0, 1, ring.device(-1, 0))

    def second(ring, i):
        q = ring.where(steps[i], 0)
        ring.send(q, 0, 4 + 4 * i, ring.device(0, 1))
        ring.send(q, 0, 5 + 4 * i, ring.device(0, -1))

    def first_near(ring, i):
        q = ring.where(steps[i], 0)
        ring.wait(q, 0, i - 1)
        ring.send(q, i, 1 + i, ring.device(-steps[i], 0))

    def first_far(ring):
        q = ring.where(2, 0)
        ring.wait(q, 1, 2)
        ring.wait(q, 2, 3)

    def second_near(ring, i):
        for n, (step, part) in enumerate(((-1, 1), (1, 2))):
            q = ring.where(steps[i], step)
            ring.wait(q, 0, 4 + 4 * i + n)
            ring.send(q, part, 6 + 4 * i + n, ring.device(0, -step))

    def second_far(ring, i):
        q = ring.where(steps[i], 2)
        ring.wait(q, 1, 6 + 4 * i)
        ring.wait(q, 2, 7 + 4 * i)

    for ring in rings:
        first_own(ring)
    for ring in rings:
        second(ring, 0)
    for i in (1, 2):
        for ring in rings:
            first_near(ring, i)
            second(ring, i)

    def top_leg(a, d):
        if a == 0:
            src, dst, device = top_a, top.at[pl.ds(0, half)], x * SIDE + d
        else:
            src, dst, device = top_b, top.at[pl.ds(half, half)], d * SIDE + y
        return remote(
            src.at[:, pl.ds(d * NB, NB)], dst,
            top_send.at[20 + 4 * a + d], top_recv.at[5 + a], {"prow": device},
        )

    @pl.when(me == 0)
    def _():
        for c in top_own:
            c.wait()

    @pl.when(y == 0)
    def _():
        @pl.when(x != 0)
        def _():
            top_x(1).wait_recv()

        for d in range(1, SIDE):
            top_leg(0, d).start()
        top[pl.ds(0, half), :] = top_a[:, pl.ds(0, NB)]

    @pl.when(x == 0)
    def _():
        @pl.when(y != 0)
        def _():
            for k in range(SIDE):
                top_y(1, k).wait_recv()

        for d in range(1, SIDE):
            top_leg(1, d).start()
        top[pl.ds(half, half), :] = top_b[:, pl.ds(0, NB)]

    for ring in rings:
        first_far(ring)
        second(ring, 3)
    for ring in rings:
        second_near(ring, 0)

    def panel_leg(h):
        @pl.when((core == 0) & (z > 0))
        def _():
            panel_next(h, 0, other).wait_recv()
            panel_next(h, 4 + h, other).start()

            @pl.when((z == 1) if h == 0 else (z == 3))
            def _():
                panel_next(h, 0, 4).start()

    panel_leg(0)
    panel_leg(1)

    @pl.when(y != 0)
    def _():
        top_leg(0, 1).wait_recv()

    @pl.when(x != 0)
    def _():
        top_leg(1, 1).wait_recv()

    def back_rows(r, carry):
        for s in range(slots):
            index = leaving[r * NB + s] & (NB - 1)
            back[pl.ds(r * slots + s, 1), :] = top[pl.ds(index, 1), :]
        return carry

    lax.fori_loop(0, PROWS, back_rows, 0)

    def ret_copy(d):
        peer = (me + d) % PROWS
        return remote(
            back.at[pl.ds(pl.multiple_of(peer * slots, 8), slots)],
            returned.at[pl.ds(0, slots), block(me)],
            ret_send.at[d], ret_recv.at[d], {"prow": peer},
        )

    def ret_start(d, carry):
        ret_copy(d).start()
        return carry

    def ret_wait(d, carry):
        peer = (me - d + PROWS) % PROWS
        remote(
            back.at[pl.ds(0, slots)], returned.at[pl.ds(0, slots), block(peer)],
            ret_send.at[d], ret_recv.at[d], {"prow": peer},
        ).wait_recv()
        return carry

    def ret_sent(d, carry):
        ret_copy(d).wait_send()
        return carry

    lax.fori_loop(1, PROWS, ret_start, 0)
    ret_own = pltpu.make_async_copy(
        back.at[pl.ds(pl.multiple_of(me * slots, 8), slots)],
        returned.at[pl.ds(0, slots), block(me)], own_sem.at[8],
    )
    ret_own.start()

    for i in (1, 2, 3):
        for ring in rings:
            second_near(ring, i)

    def inv_copy(k, device):
        return remote(inverse, inverse, inv_send.at[k], inv_recv.at[0], device)

    @pl.when(col == 0)
    def _():
        @pl.when(me != 0)
        def _():
            inv_copy(0, {"pcol": other}).wait_recv()

        @pl.when(me == 0)
        def _():
            for d in range(1, SIDE):
                inv_copy(d, {"prow": d * SIDE}).start()

        @pl.when(y == 0)
        def _():
            for d in range(1, SIDE):
                inv_copy(3 + d, {"prow": x * SIDE + d}).start()

        inv_copy(7, {"pcol": z_up}).start()
        inv_copy(8, {"pcol": z_down}).start()
        inv_copy(9, {"pcol": other}).start()

    @pl.when(col != 0)
    def _():
        inv_copy(0, {"pcol": other}).wait_recv()

        @pl.when(core == 0)
        def _():
            inv_copy(9, {"pcol": other}).start()

            @pl.when(z == 1)
            def _():
                inv_copy(7, {"pcol": 4}).start()

    for i in range(4):
        for ring in rings:
            second_far(ring, i)
    lax.fori_loop(1, PROWS, ret_wait, 0)
    ret_own.wait()

    @pl.when(core == 1)
    def _():
        panel_next(0, 0, other).wait_recv()
        panel_next(1, 0, other).wait_recv()

    for c in sent:
        c.wait_send()
    lax.fori_loop(1, PROWS, row_sent, 0)
    lax.fori_loop(1, PROWS, ret_sent, 0)

    @pl.when(me == 0)
    def _():
        for d in (1, 3, 2):
            top_x(d).wait_send()
            for k in range(SIDE):
                top_y(d, k).wait_send()

    @pl.when(y == 0)
    def _():
        for d in range(1, SIDE):
            top_leg(0, d).wait_send()

    @pl.when(x == 0)
    def _():
        for d in range(1, SIDE):
            top_leg(1, d).wait_send()

    @pl.when(col == 0)
    def _():
        panel_own.wait()
        for h, k in ((0, 0), (1, 1), (1, 2), (0, 3), (0, 4), (1, 5)):
            panel_first(h, k, other).wait_send()

        @pl.when(me == 0)
        def _():
            for d in range(1, SIDE):
                inv_copy(d, {"prow": d * SIDE}).wait_send()

        @pl.when(y == 0)
        def _():
            for d in range(1, SIDE):
                inv_copy(3 + d, {"prow": x * SIDE + d}).wait_send()

        for k in (7, 8, 9):
            inv_copy(k, {"pcol": other}).wait_send()

    @pl.when((core == 0) & (z > 0))
    def _():
        panel_next(0, 4, other).wait_send()
        panel_next(1, 5, other).wait_send()
        inv_copy(9, {"pcol": other}).wait_send()

        @pl.when(z == 1)
        def _():
            panel_next(0, 0, other).wait_send()
            inv_copy(7, {"pcol": other}).wait_send()

        @pl.when(z == 3)
        def _():
            panel_next(1, 0, other).wait_send()


def exchange(slots, collective_id, owner, slot, leaving, matrix, picks):
    rows_dev, cols_dev = matrix.shape
    f32 = jnp.float32
    smem = pl.BlockSpec(memory_space=pltpu.SMEM)
    vmem = pl.BlockSpec(memory_space=pltpu.VMEM)
    anywhere = pl.BlockSpec(memory_space=pl.ANY)
    dma = pltpu.SemaphoreType.DMA
    return pl.pallas_call(
        functools.partial(exchange_kernel, slots),
        out_shape=[
            jax.ShapeDtypeStruct((NB, cols_dev), f32),
            jax.ShapeDtypeStruct((rows_dev, NB), f32),
            jax.ShapeDtypeStruct((NB, NB), f32),
            jax.ShapeDtypeStruct((NB, cols_dev), f32),
        ],
        in_specs=[smem, smem, smem, anywhere, anywhere],
        out_specs=[vmem, vmem, vmem, anywhere],
        scratch_shapes=[
            pltpu.VMEM((PROWS * slots, NB), f32),
            pltpu.VMEM((NB, NB), f32),
            pltpu.VMEM((NB, NB), f32),
            pltpu.VMEM((NB // 2, SIDE * NB), f32),
            pltpu.VMEM((NB // 2, SIDE * NB), f32),
            pltpu.VMEM((PROWS * slots, NB), f32),
            pltpu.VMEM((NB, NB), f32),
            dma((PROWS,)), dma((PROWS,)), dma((PROWS,)), dma((PROWS,)),
            dma((2, 20)), dma((2, 20)),
            dma((28,)), dma((7,)), dma((6,)), dma((2,)), dma((10,)), dma((1,)), dma((9,)),
        ],
        compiler_params=pltpu.CompilerParams(
            collective_id=collective_id, has_side_effects=True, vmem_limit_bytes=VMEM_BYTES
        ),
        name="exchange_%d" % slots,
    )(owner, slot, leaving, matrix, picks)


def split(value):
    high = value.astype(jnp.bfloat16)
    return high, (value - high.astype(jnp.float32)).astype(jnp.bfloat16)


def update_kernel(
    place, info, matrix, gathered, panel, inverse, returned, out,
    factor, chosen, chosen_factor, fixed,
):
    rows_dev = matrix.shape[0]
    step = pl.program_id(0)
    me = lax.axis_index("prow")
    col = lax.axis_index("pcol")
    owned = info[0]

    def stacked(value):
        high, low = split(value)
        return jnp.concatenate([high, low, high], axis=1)

    @pl.when(step == 0)
    def _():
        factor[...] = stacked(panel[...])

        def choose(s, carry):
            p = jnp.maximum(place[s], 0)
            chosen[pl.ds(s, 1), :] = panel[pl.ds(p, 1), :]
            return carry

        lax.fori_loop(0, owned, choose, 0)
        chosen_factor[...] = stacked(chosen[...])

    upper = jnp.dot(
        inverse[...], gathered[...], precision=HIGHEST, preferred_element_type=jnp.float32
    )
    high, low = split(upper)
    terms = jnp.concatenate([high, high, low], axis=0)
    out[...] = matrix[...] - jnp.dot(factor[...], terms, preferred_element_type=jnp.float32)

    def put(size):
        fixed[pl.ds(0, size), :] = returned[pl.ds(0, size), :] - jnp.dot(
            chosen_factor[pl.ds(0, size), :], terms, preferred_element_type=jnp.float32
        )

    @pl.when(owned <= 32)
    def _():
        put(32)

    @pl.when(owned > 32)
    def _():
        put(NB)

    def fix(s, carry):
        @pl.when(place[s] >= 0)
        def _():
            out[pl.ds(place[s], 1), :] = fixed[pl.ds(s, 1), :]

        return carry

    lax.fori_loop(0, owned, fix, 0)

    @pl.when(me == 0)
    def _():
        out[pl.ds(0, NB), :] = upper

    @pl.when((col == 0) & (step == 0))
    def _():
        out[:, pl.ds(0, NB)] = matrix[:, pl.ds(0, NB)]


def update(place, info, matrix, gathered, panel, inverse, returned):
    rows_dev, cols_dev = matrix.shape
    wide = 256
    smem = pl.BlockSpec(memory_space=pltpu.SMEM)

    def columns(rows):
        return pl.BlockSpec((rows, wide), lambda i: (0, i))

    def whole(rows):
        return pl.BlockSpec((rows, NB), lambda i: (0, 0))

    return pl.pallas_call(
        update_kernel,
        grid=(cols_dev // wide,),
        out_shape=jax.ShapeDtypeStruct(matrix.shape, jnp.float32),
        in_specs=[
            smem, smem, columns(rows_dev), columns(NB), whole(rows_dev), whole(NB), columns(NB)
        ],
        out_specs=columns(rows_dev),
        scratch_shapes=[
            pltpu.VMEM((rows_dev, 3 * NB), jnp.bfloat16),
            pltpu.VMEM((NB, NB), jnp.float32),
            pltpu.VMEM((NB, 3 * NB), jnp.bfloat16),
            pltpu.VMEM((NB, wide), jnp.float32),
        ],
        compiler_params=pltpu.CompilerParams(vmem_limit_bytes=VMEM_BYTES),
        name="update",
    )(place, info, matrix, gathered, panel, inverse, returned)


def plan(matrix, pivots):
    i32 = jnp.int32
    smem = pl.BlockSpec(memory_space=pltpu.SMEM)
    anywhere = pl.BlockSpec(memory_space=pl.ANY)
    return pl.pallas_call(
        plan_kernel,
        out_shape=[
            jax.ShapeDtypeStruct((NB, matrix.shape[1]), jnp.float32),
            jax.ShapeDtypeStruct((NB,), i32),
            jax.ShapeDtypeStruct((NB,), i32),
            jax.ShapeDtypeStruct((PROWS * NB,), i32),
            jax.ShapeDtypeStruct((NB,), i32),
            jax.ShapeDtypeStruct((8,), i32),
        ],
        in_specs=[smem, anywhere],
        out_specs=[anywhere, smem, smem, smem, smem, smem],
        scratch_shapes=[
            pltpu.SMEM((PROWS * matrix.shape[0],), i32),
            pltpu.SMEM((PROWS,), i32),
            pltpu.SemaphoreType.DMA((NB,)),
        ],
        compiler_params=pltpu.CompilerParams(vmem_limit_bytes=VMEM_BYTES),
        name="plan",
    )(pivots, matrix)


def local(matrix, pivots):
    picks, owner, slot, leaving, place, info = plan(matrix, pivots)
    gathered, panel, inverse, returned = lax.cond(
        info[1] <= FEW,
        functools.partial(exchange, FEW, 0),
        functools.partial(exchange, NB, 1),
        owner, slot, leaving, matrix, picks,
    )
    return update(place, info, matrix, gathered, panel, inverse, returned)


def solution(mesh):
    placed = (P("prow", "pcol"), P())
    return jax.shard_map(
        local, mesh=mesh, in_specs=placed, out_specs=P("prow", "pcol"), check_vma=False
    )
```

time: 483 us -> 61.4 us (0.13)
  the two profiles are of different devices: /device:TPU:0 before, /device:TPU:85 now
where the time goes in v1:
time: 61.4 us; the launch traced here: 60.9 us
  Pallas kernels  59 us (96%)
  local copies, waits for them, and re-layouts  1.24 us (2%)
  between operations  0.67 us (1%)
    pallas_call x1, Pallas kernels, exchange(): pl.pallas_call(functools.partial(exchange_kernel, slots), out_shape=[jax....  40.4 us
    pallas_call x1, Pallas kernels, update(): pl.pallas_call(update_kernel, grid=(cols_dev // wide,), out_shape=jax.Sha...  12.9 us
    pallas_call x1, Pallas kernels, plan(): pl.pallas_call(plan_kernel, out_shape=[jax.ShapeDtypeStruct((NB, matrix.s...  5.64 us
    slice x1, local copies, waits for them, and re-layouts, local(): info[1] <= FEW  1.24 us

profile of v1, /device:TPU:85, one launch (start us, length us, event | category | flops | bytes accessed | tf_op | source)
XLA Modules:
  0.0 60.9 jit_solution(11716775286521905777)
XLA Ops:
  0.0 5.6 %plan.1 = (f32[128,2048]{1,0:T(8,128)S(1)}, s32[128]{0:T(128)S(1)}, s32[128]{0:T(128)S(1)}, s32[2048]{0:T(1024)S(1)}, s32[128]{0:T(128)}, /*index=5*/s32[8]{0:T(128)}) custom-call(s32[128]{0:T(128)} %pivots.1, f32[1024,2048]{1,0:T(8,128)} %matrix.3), custom_call_target="tpu_custom_call" | custom-call | tf_op jit(solution)/shard_map/plan/pallas_call | solution.py:663
  5.6 1.2 %slice.3 = s32[1]{0:T(128)} slice(s32[8]{0:T(128)} %get-tuple-element.46.info), slice={[1:2]} | slice | bytes 8 | tf_op jit(solution)/shard_map/slice | solution.py:688
  7.5 40.4 %conditional.1 = ((f32[128,2048]{1,0:T(8,128)S(1)}, f32[1024,128]{1,0:T(8,128)}, f32[128,128]{1,0:T(8,128)S(1)}, f32[128,2048]{1,0:T(8,128)S(1)})) conditional(s32[]{:T(128)} %bitcast, (s32[128]{0:T(128)S(1)}, s32[128]{0:T(128)S(1)}, s32[2048]{0:T(1024)S(1)}, f32[1024,2048]{1,0:T(8,128)}, f32[128,2048]{1,0:T(8,128)S(1)}) %tuple.11, ...), branch_computations={%region_0.0_spmd, %region_1.0_spmd} | conditional | bytes 8 | solution.py:687
  7.6 40.4 %exchange_24.1 = (f32[128,2048]{1,0:T(8,128)S(1)}, f32[1024,128]{1,0:T(8,128)}, f32[128,128]{1,0:T(8,128)S(1)}, f32[128,2048]{1,0:T(8,128)S(1)}) custom-call(s32[128]{0:T(128)S(1)} %get-tuple-element.30.owner, s32[128]{0:T(128)S(1)} %get-tuple-element.31.slot, s32[2048]{0:T(1024)S(1)} %get-tuple-element.32.leaving, f32[1024,2048]{1,0:T(8,128)} %get-tuple-element.33.matrix, ...), custom_call_target="tpu_custom_call" | custom-call | tf_op jit(solution)/shard_map/cond/branch_1_fun/exchange_24/pallas_call | solution.py:531
  48.0 12.9 %update.1 = f32[1024,2048]{1,0:T(8,128)} custom-call(s32[128]{0:T(128)} %get-tuple-element.45.place, s32[8]{0:T(128)} %get-tuple-element.46.info, f32[1024,2048]{1,0:T(8,128)} %matrix.3, f32[128,2048]{1,0:T(8,128)S(1)} %get-tuple-element.51.gathered, f32[1024,128]{1,0:T(8,128)} %get-tuple-element.52.panel, f32[128,128]{1,0:T(8,128)S(1)} %get-tuple-element.53.inverse, ...), custom_call_target="tpu_custom_call" | custom-call | tf_op jit(solution)/shard_map/update/pallas_call | solution.py:640

commit v2 on v1

v2 whole, which is shorter than its diff:
```python
import functools

import jax
import jax.numpy as jnp
from jax import lax
from jax.experimental import pallas as pl
from jax.experimental.pallas import tpu as pltpu
from jax.sharding import PartitionSpec as P

NB = 128
PROWS = 16
SIDE = 4
FEW = 24
MIB = 1024 * 1024
LOADS = 8
WIDE = 256
HIGHEST = lax.Precision.HIGHEST


def invert_unit_lower(block):
    rows = lax.broadcasted_iota(jnp.int32, (NB, NB), 0)
    cols = lax.broadcasted_iota(jnp.int32, (NB, NB), 1)
    eye = jnp.where(rows == cols, 1.0, 0.0).astype(jnp.float32)
    dot = functools.partial(jnp.dot, precision=HIGHEST, preferred_element_type=jnp.float32)
    inverse = eye
    size = 1
    while size < NB:
        corner = (rows // size == cols // size + 1) & (rows // (2 * size) == cols // (2 * size))
        part = jnp.where(corner, block, 0.0)
        if size == 1:
            inverse = eye - part
        else:
            inverse = inverse - dot(dot(inverse, part), inverse)
        size *= 2
    return inverse


def swap_plan(slots, pivots, me, rows_dev, table):
    shape = (NB, NB)
    down = lax.broadcasted_iota(jnp.int32, shape, 0)
    over = lax.broadcasted_iota(jnp.int32, shape, 1)
    earlier = over < down

    def as_row(column):
        return jnp.sum(jnp.where(down == over, column, 0), axis=0, keepdims=True)

    def as_column(row):
        return jnp.sum(jnp.where(down == over, row, 0), axis=1, keepdims=True)

    def look_up(row, index):
        return jnp.sum(jnp.where(over == index, row, 0), axis=1, keepdims=True)

    def last(where):
        return jnp.max(jnp.where(where, over, -1), axis=1, keepdims=True)

    p_row = pivots[...]
    p_col = as_column(p_row)
    steps = lax.broadcasted_iota(jnp.int32, (NB, 1), 0)
    touched = last((p_row == down) & earlier)
    held = jnp.where(touched >= 0, touched, steps)
    for _ in range(7):
        held = look_up(as_row(held), held)
    held_row = as_row(held)
    same = p_row == p_col
    before = last(same & earlier)
    source = jnp.where(before >= 0, look_up(held_row, before), p_col)
    leaves = look_up(held_row, last(same))
    owner = source // rows_dev
    slot = jnp.sum(
        jnp.where((as_row(owner) == owner) & earlier, 1, 0), axis=1, keepdims=True
    )
    code = owner * slots + jnp.minimum(slot, slots - 1)
    mine = (owner == me) & (slot == over)
    offset = source - me * rows_dev
    wide = lax.broadcasted_iota(jnp.int32, (NB, PROWS * slots), 1)
    code_wide = owner * slots + slot
    hit = (code_wide == wide) & (slot < slots)
    table[pl.ds(0, 1), pl.ds(0, NB)] = as_row(code)
    table[pl.ds(1, 1), pl.ds(0, NB)] = jnp.sum(
        jnp.where(mine, offset, 0), axis=0, keepdims=True
    )
    table[pl.ds(2, 1), pl.ds(0, NB)] = (
        jnp.sum(jnp.where(mine & (source >= NB), offset + 1, 0), axis=0, keepdims=True) - 1
    )
    table[pl.ds(3, 1), :] = jnp.sum(jnp.where(hit, leaves, 0), axis=0, keepdims=True)
    table[pl.ds(4, 1), pl.ds(0, NB)] = as_row(slot)


def exchange_kernel(
    slots,
    pivots, matrix,
    resident, gathered, panel, inverse, returned, place, most,
    table, plan, picks, received, ordered, top, top_a, top_b, back, corner,
    row_send, row_recv, ret_send, ret_recv, ring_send, ring_recv,
    top_send, top_recv, panel_send, panel_recv, inv_send, inv_recv, own_sem, load_sem,
):
    half = NB // 2
    rows_dev = matrix.shape[0]
    me = lax.axis_index("prow")
    col = lax.axis_index("pcol")
    x, y = me // SIDE, me % SIDE
    z, core = col // 2, col % 2
    sent = []

    def block(q):
        return pl.ds(pl.multiple_of(q * NB, NB), NB)

    def remote(src, dst, send_sem, recv_sem, device):
        return pltpu.make_async_remote_copy(
            src_ref=src, dst_ref=dst, send_sem=send_sem, recv_sem=recv_sem, device_id=device
        )

    z_up, z_down = ((z + 1) % 4) * 2 + core, ((z + 3) % 4) * 2 + core
    other = z * 2 + 1 - core
    barrier = pltpu.get_barrier_semaphore()
    for d in range(1, PROWS):
        pl.semaphore_signal(barrier, inc=1, device_id={"prow": (me + d) % PROWS})
    for c in (z_up, z_down, other):
        pl.semaphore_signal(barrier, inc=1, device_id={"pcol": c})
    pl.semaphore_wait(barrier, PROWS - 1 + 3)

    def top_x(d):
        return remote(
            matrix.at[pl.ds(0, half), pl.ds(d * SIDE * NB, SIDE * NB)], top_a,
            top_send.at[d], top_recv.at[0], {"prow": d * SIDE},
        )

    def top_y(d, k):
        return remote(
            matrix.at[pl.ds(half, half), pl.ds((k * SIDE + d) * NB, NB)],
            top_b.at[:, pl.ds(k * NB, NB)],
            top_send.at[4 + 4 * d + k], top_recv.at[1 + k], {"prow": d},
        )

    top_own = [
        pltpu.make_async_copy(
            matrix.at[pl.ds(0, half), pl.ds(0, SIDE * NB)], top_a, own_sem.at[1]
        )
    ] + [
        pltpu.make_async_copy(
            matrix.at[pl.ds(half, half), pl.ds(k * SIDE * NB, NB)],
            top_b.at[:, pl.ds(k * NB, NB)], own_sem.at[2 + k],
        )
        for k in range(SIDE)
    ]
    diagonal = pltpu.make_async_copy(matrix.at[pl.ds(0, NB), pl.ds(0, NB)], corner, own_sem.at[6])

    @pl.when(me == 0)
    def _():
        for d in (1, 3, 2):
            top_x(d).start()
            for k in range(SIDE):
                top_y(d, k).start()
        for c in top_own:
            c.start()

    @pl.when((me == 0) & (col == 0))
    def _():
        diagonal.start()

    halves = [pl.ds(0, rows_dev // 2), pl.ds(rows_dev // 2, rows_dev // 2)]
    first_panel = matrix.at[:, pl.ds(0, NB)]

    def panel_first(h, k, to):
        return remote(
            first_panel.at[halves[h]], panel.at[halves[h]],
            panel_send.at[k], panel_recv.at[h], {"pcol": to},
        )

    def panel_next(h, k, to):
        return remote(
            panel.at[halves[h]], panel.at[halves[h]],
            panel_send.at[k], panel_recv.at[h], {"pcol": to},
        )

    panel_own = pltpu.make_async_copy(first_panel, panel, own_sem.at[7])

    @pl.when(col == 0)
    def _():
        panel_first(0, 0, z_up).start()
        panel_first(1, 1, z_down).start()
        panel_first(1, 2, z_up).start()
        panel_first(0, 3, z_down).start()
        panel_first(0, 4, other).start()
        panel_first(1, 5, other).start()
        panel_own.start()

    loads = []
    for k in range(LOADS):
        part = pl.ds(k * (rows_dev // LOADS), rows_dev // LOADS)
        loads.append(
            pltpu.make_async_copy(matrix.at[part, :], resident.at[part, :], load_sem.at[k])
        )
        loads[-1].start()

    swap_plan(slots, pivots, me, rows_dev, table)
    plan_copy = pltpu.make_async_copy(table, plan, own_sem.at[9])
    plan_copy.start()
    place[...] = table[pl.ds(2, 1), pl.ds(0, NB)]
    plan_copy.wait()
    for c in loads:
        c.wait()

    def pick(s, carry):
        picks[pl.ds(s, 1), :] = resident[pl.ds(plan[1, s], 1), :]
        return carry

    lax.fori_loop(0, slots, pick, 0, unroll=4)

    def row_copy(d):
        peer = (me + d) % PROWS
        return remote(
            picks.at[:, block(peer)],
            received.at[pl.ds(pl.multiple_of(me * slots, 8), slots)],
            row_send.at[d], row_recv.at[d], {"prow": peer},
        )

    def row_start(d, carry):
        row_copy(d).start()
        return carry

    def row_wait(d, carry):
        row_copy(d).wait_recv()
        return carry

    def row_sent(d, carry):
        row_copy(d).wait_send()
        return carry

    lax.fori_loop(1, PROWS, row_start, 0)

    def inv_copy(k, device):
        return remote(inverse, inverse, inv_send.at[k], inv_recv.at[0], device)

    @pl.when((me == 0) & (col == 0))
    def _():
        diagonal.wait()
        inverse[...] = invert_unit_lower(corner[...])
        for d in range(1, SIDE):
            inv_copy(d, {"prow": d * SIDE}).start()

    own_rows = pltpu.make_async_copy(
        picks.at[:, block(me)],
        received.at[pl.ds(pl.multiple_of(me * slots, 8), slots)],
        own_sem.at[0],
    )
    own_rows.start()
    own_rows.wait()
    lax.fori_loop(1, PROWS, row_wait, 0)

    def order(j, carry):
        ordered[pl.ds(j, 1), :] = received[pl.ds(plan[0, j], 1), :]
        return carry

    lax.fori_loop(0, NB, order, 0, unroll=8)
    gathered[:, block(me)] = ordered[...]

    def spot(o, along, across):
        dx, dy = (along, across) if o == 0 else (across, along)
        return ((x + dx + SIDE) % SIDE) * SIDE + (y + dy + SIDE) % SIDE

    def ring_copy(o, q, sem, device):
        ref = gathered.at[pl.ds(o * half, half), block(q)]
        return remote(ref, ref, ring_send.at[o, sem], ring_recv.at[o, sem], {"prow": device})

    def ring_start(o, q, sem, device):
        c = ring_copy(o, q, sem, device)
        c.start()
        sent.append(c)

    for d in (2, 1, 3):
        for o in (0, 1):
            ring_start(o, me, d, spot(o, d, 0))
    for d in (2, 1, 3):
        for o in (0, 1):
            ring_start(o, me, 3 + d, spot(o, 0, d))

    def top_leg(a, d):
        if a == 0:
            src, dst, device = top_a, top.at[pl.ds(0, half)], x * SIDE + d
        else:
            src, dst, device = top_b, top.at[pl.ds(half, half)], d * SIDE + y
        return remote(
            src.at[:, pl.ds(d * NB, NB)], dst,
            top_send.at[20 + 4 * a + d], top_recv.at[5 + a], {"prow": device},
        )

    @pl.when(me == 0)
    def _():
        for c in top_own:
            c.wait()

    @pl.when(y == 0)
    def _():
        @pl.when(x != 0)
        def _():
            top_x(1).wait_recv()

        for d in range(1, SIDE):
            top_leg(0, d).start()
        top[pl.ds(0, half), :] = top_a[:, pl.ds(0, NB)]

    @pl.when(x == 0)
    def _():
        @pl.when(y != 0)
        def _():
            for k in range(SIDE):
                top_y(1, k).wait_recv()

        for d in range(1, SIDE):
            top_leg(1, d).start()
        top[pl.ds(half, half), :] = top_b[:, pl.ds(0, NB)]

    for e in (1, 3, 2):
        for o in (0, 1):
            q = spot(o, -e, 0)
            ring_copy(o, q, e, me).wait_recv()
            for d in (2, 1, 3):
                ring_start(o, q, 3 + 3 * e + d, spot(o, 0, d))

    @pl.when((col == 0) & (y == 0))
    def _():
        @pl.when(x != 0)
        def _():
            inv_copy(0, {"pcol": other}).wait_recv()

        for d in range(1, SIDE):
            inv_copy(3 + d, {"prow": x * SIDE + d}).start()

    def panel_leg(h):
        @pl.when((core == 0) & (z > 0))
        def _():
            panel_next(h, 0, other).wait_recv()
            panel_next(h, 4 + h, other).start()

            @pl.when((z == 1) if h == 0 else (z == 3))
            def _():
                panel_next(h, 0, 4).start()

    panel_leg(0)
    panel_leg(1)

    @pl.when(y != 0)
    def _():
        top_leg(0, 1).wait_recv()

    @pl.when(x != 0)
    def _():
        top_leg(1, 1).wait_recv()

    def back_rows(r, carry):
        for s in range(slots):
            index = plan[3, r * slots + s]
            back[pl.ds(r * slots + s, 1), :] = top[pl.ds(index, 1), :]
        return carry

    lax.fori_loop(0, PROWS, back_rows, 0)

    def ret_copy(d):
        peer = (me + d) % PROWS
        return remote(
            back.at[pl.ds(pl.multiple_of(peer * slots, 8), slots)],
            returned.at[:, block(me)],
            ret_send.at[d], ret_recv.at[d], {"prow": peer},
        )

    def ret_start(d, carry):
        ret_copy(d).start()
        return carry

    def ret_wait(d, carry):
        peer = (me - d + PROWS) % PROWS
        remote(
            back.at[pl.ds(0, slots)], returned.at[:, block(peer)],
            ret_send.at[d], ret_recv.at[d], {"prow": peer},
        ).wait_recv()
        return carry

    def ret_sent(d, carry):
        ret_copy(d).wait_send()
        return carry

    lax.fori_loop(1, PROWS, ret_start, 0)
    ret_own = pltpu.make_async_copy(
        back.at[pl.ds(pl.multiple_of(me * slots, 8), slots)],
        returned.at[:, block(me)], own_sem.at[8],
    )
    ret_own.start()

    @pl.when(col == 0)
    def _():
        @pl.when(y != 0)
        def _():
            inv_copy(0, {"pcol": other}).wait_recv()

        inv_copy(7, {"pcol": z_up}).start()
        inv_copy(8, {"pcol": z_down}).start()
        inv_copy(9, {"pcol": other}).start()

    for e in (0, 1, 3, 2):
        for d in (1, 3, 2):
            for o in (0, 1):
                ring_copy(o, spot(o, -e, -d), 3 + 3 * e + d, me).wait_recv()

    @pl.when(col != 0)
    def _():
        inv_copy(0, {"pcol": other}).wait_recv()

        @pl.when(core == 0)
        def _():
            inv_copy(9, {"pcol": other}).start()

            @pl.when(z == 1)
            def _():
                inv_copy(7, {"pcol": 4}).start()

    most[0] = lax.fori_loop(0, NB, lambda j, m: jnp.maximum(m, plan[4, j]), 0, unroll=8)
    lax.fori_loop(1, PROWS, ret_wait, 0)
    ret_own.wait()

    @pl.when(core == 1)
    def _():
        panel_next(0, 0, other).wait_recv()
        panel_next(1, 0, other).wait_recv()

    for c in sent:
        c.wait_send()
    lax.fori_loop(1, PROWS, row_sent, 0)
    lax.fori_loop(1, PROWS, ret_sent, 0)

    @pl.when(me == 0)
    def _():
        for d in (1, 3, 2):
            top_x(d).wait_send()
            for k in range(SIDE):
                top_y(d, k).wait_send()

    @pl.when(y == 0)
    def _():
        for d in range(1, SIDE):
            top_leg(0, d).wait_send()

    @pl.when(x == 0)
    def _():
        for d in range(1, SIDE):
            top_leg(1, d).wait_send()

    @pl.when(col == 0)
    def _():
        panel_own.wait()
        for h, k in ((0, 0), (1, 1), (1, 2), (0, 3), (0, 4), (1, 5)):
            panel_first(h, k, other).wait_send()

        @pl.when(me == 0)
        def _():
            for d in range(1, SIDE):
                inv_copy(d, {"prow": d * SIDE}).wait_send()

        @pl.when(y == 0)
        def _():
            for d in range(1, SIDE):
                inv_copy(3 + d, {"prow": x * SIDE + d}).wait_send()

        for k in (7, 8, 9):
            inv_copy(k, {"pcol": other}).wait_send()

    @pl.when((core == 0) & (z > 0))
    def _():
        panel_next(0, 4, other).wait_send()
        panel_next(1, 5, other).wait_send()
        inv_copy(9, {"pcol": other}).wait_send()

        @pl.when(z == 1)
        def _():
            panel_next(0, 0, other).wait_send()
            inv_copy(7, {"pcol": other}).wait_send()

        @pl.when(z == 3)
        def _():
            panel_next(1, 0, other).wait_send()


def exchange(slots, collective_id, matrix, pivots):
    rows_dev, cols_dev = matrix.shape
    f32, i32 = jnp.float32, jnp.int32
    smem = pl.BlockSpec(memory_space=pltpu.SMEM)
    vmem = pl.BlockSpec(memory_space=pltpu.VMEM)
    hbm = pl.BlockSpec(memory_space=pltpu.HBM)
    dma = pltpu.SemaphoreType.DMA
    return pl.pallas_call(
        functools.partial(exchange_kernel, slots),
        out_shape=[
            pltpu.VMEM((rows_dev, cols_dev), f32),
            jax.ShapeDtypeStruct((NB, cols_dev), f32),
            jax.ShapeDtypeStruct((rows_dev, NB), f32),
            jax.ShapeDtypeStruct((NB, NB), f32),
            jax.ShapeDtypeStruct((slots, cols_dev), f32),
            jax.ShapeDtypeStruct((1, NB), i32),
            jax.ShapeDtypeStruct((1,), i32),
        ],
        in_specs=[vmem, hbm],
        out_specs=[vmem, vmem, vmem, vmem, vmem, vmem, smem],
        scratch_shapes=[
            pltpu.VMEM((8, PROWS * slots), i32),
            pltpu.SMEM((8, PROWS * slots), i32),
            pltpu.VMEM((slots, cols_dev), f32),
            pltpu.VMEM((PROWS * slots, NB), f32),
            pltpu.VMEM((NB, NB), f32),
            pltpu.VMEM((NB, NB), f32),
            pltpu.VMEM((NB // 2, SIDE * NB), f32),
            pltpu.VMEM((NB // 2, SIDE * NB), f32),
            pltpu.VMEM((PROWS * slots, NB), f32),
            pltpu.VMEM((NB, NB), f32),
            dma((PROWS,)), dma((PROWS,)), dma((PROWS,)), dma((PROWS,)),
            dma((2, 16)), dma((2, 16)),
            dma((28,)), dma((7,)), dma((6,)), dma((2,)), dma((10,)), dma((1,)), dma((10,)),
            dma((LOADS,)),
        ],
        compiler_params=pltpu.CompilerParams(
            collective_id=collective_id, has_side_effects=True, vmem_limit_bytes=24 * MIB
        ),
        name="exchange_%d" % slots,
    )(pivots, pltpu.with_memory_space_constraint(matrix, pltpu.HBM))


def split(value):
    high = value.astype(jnp.bfloat16)
    return high, (value - high.astype(jnp.float32)).astype(jnp.bfloat16)


def stacked(value):
    high, low = split(value)
    return jnp.concatenate([high, low, high], axis=1)


def update_kernel(
    slots, place, matrix, gathered, panel, inverse, returned, out,
    result, factor, chosen, chosen_factor, fixed, sems,
):
    me = lax.axis_index("prow")
    col = lax.axis_index("pcol")
    factor[...] = stacked(panel[...])

    def choose(s, carry):
        p = jnp.maximum(place[0, s], 0)
        chosen[pl.ds(s, 1), :] = panel[pl.ds(p, 1), :]
        return carry

    lax.fori_loop(0, slots, choose, 0, unroll=4)
    chosen_factor[...] = stacked(chosen[...])

    def write(n):
        return pltpu.make_async_copy(
            result.at[:, pl.ds(n * WIDE, WIDE)], out.at[:, pl.ds(n * WIDE, WIDE)], sems.at[n]
        )

    parts = matrix.shape[1] // WIDE
    for n in range(parts):
        here = pl.ds(n * WIDE, WIDE)
        upper = jnp.dot(
            inverse[...], gathered[:, here], precision=HIGHEST, preferred_element_type=jnp.float32
        )
        high, low = split(upper)
        terms = jnp.concatenate([high, high, low], axis=0)
        result[:, here] = matrix[:, here] - jnp.dot(
            factor[...], terms, preferred_element_type=jnp.float32
        )
        fixed[...] = returned[:, here] - jnp.dot(
            chosen_factor[...], terms, preferred_element_type=jnp.float32
        )

        def fix(s, carry):
            @pl.when(place[0, s] >= 0)
            def _():
                result[pl.ds(place[0, s], 1), here] = fixed[pl.ds(s, 1), :]

            return carry

        lax.fori_loop(0, slots, fix, 0)

        @pl.when(me == 0)
        def _():
            result[pl.ds(0, NB), here] = upper

        if n == 0:

            @pl.when(col == 0)
            def _():
                result[:, pl.ds(0, NB)] = matrix[:, pl.ds(0, NB)]

        write(n).start()
    for n in range(parts):
        write(n).wait()


def update(slots, matrix, gathered, panel, inverse, returned, place):
    rows_dev, cols_dev = matrix.shape
    smem = pl.BlockSpec(memory_space=pltpu.SMEM)
    vmem = pl.BlockSpec(memory_space=pltpu.VMEM)
    return pl.pallas_call(
        functools.partial(update_kernel, slots),
        out_shape=pltpu.HBM(matrix.shape, jnp.float32),
        in_specs=[smem, vmem, vmem, vmem, vmem, vmem],
        out_specs=pl.BlockSpec(memory_space=pltpu.HBM),
        scratch_shapes=[
            pltpu.VMEM((rows_dev, cols_dev), jnp.float32),
            pltpu.VMEM((rows_dev, 3 * NB), jnp.bfloat16),
            pltpu.VMEM((slots, NB), jnp.float32),
            pltpu.VMEM((slots, 3 * NB), jnp.bfloat16),
            pltpu.VMEM((slots, WIDE), jnp.float32),
            pltpu.SemaphoreType.DMA((cols_dev // WIDE,)),
        ],
        compiler_params=pltpu.CompilerParams(vmem_limit_bytes=28 * MIB),
        name="update_%d" % slots,
    )(place, matrix, gathered, panel, inverse, returned)


def local(matrix, pivots):
    pivots = pivots.reshape(1, NB)
    *found, most = exchange(FEW, 0, matrix, pivots)

    def many():
        *found, _ = exchange(NB, 1, matrix, pivots)
        return update(NB, *found)

    return lax.cond(most[0] < FEW, lambda: update(FEW, *found), many)


def solution(mesh):
    placed = (P("prow", "pcol"), P())
    return jax.shard_map(
        local, mesh=mesh, in_specs=placed, out_specs=P("prow", "pcol"), check_vma=False
    )
```

time: 61.4 us -> 50.8 us (0.83)
  the two profiles are of different devices: /device:TPU:85 before, /device:TPU:64 now
where the time goes in v2:
time: 50.8 us; the launch traced here: 50.6 us
  Pallas kernels  49.7 us (98%)
  between operations  0.74 us (1%)
    pallas_call x1, Pallas kernels, exchange(): pl.pallas_call(functools.partial(exchange_kernel, slots), out_shape=[pltp...  37.3 us
    pallas_call x1, Pallas kernels, update(): pl.pallas_call(functools.partial(update_kernel, slots), out_shape=pltpu.H...  12.4 us

profile of v2, /device:TPU:64, one launch (start us, length us, event | category | flops | bytes accessed | tf_op | source)
XLA Modules:
  0.0 50.6 jit_solution(18438798702485544216)
XLA Ops:
  0.0 0.0 copy-start
  0.0 37.3 %exchange_24.1 = (f32[1024,2048]{1,0:T(8,128)S(1)}, f32[128,2048]{1,0:T(8,128)S(1)}, f32[1024,128]{1,0:T(8,128)S(1)}, f32[128,128]{1,0:T(8,128)S(1)}, f32[24,204...) custom-call(s32[1,128]{1,0:T(1,128)} %bitcast.2, f32[1024,2048]{1,0:T(8,128)} %matrix.1), custom_call_target="tpu_custom_call" | custom-call | tf_op jit(solution)/shard_map/exchange_24/pallas_call | solution.py:490
  37.9 0.0 copy-done
  37.9 12.6 %conditional.1 = (f32[1024,2048]{1,0:T(8,128)}) conditional(s32[]{:T(128)} %bitcast.1, (s32[1,128]{1,0:T(1,128)S(1)}, f32[1024,2048]{1,0:T(8,128)}) %tuple.17, (s32[1,128]{1,0:T(1,128)S(1)}, f32[1024,2048]{1,0:T(8,128)S(1)}, f32[128,2048]{1,0:T(8,128)S(1)}, f32[1024,128]{1,0:T(8,128)S(1)}, f32[128,128]{1,0:T(8,128)S(1)}, ...), branch_computations={%region_0.0_spmd, %region_1.0_spmd} | conditional | bytes 8 | solution.py:626
  38.1 12.4 %update_24.1 = f32[1024,2048]{1,0:T(8,128)} custom-call(s32[1,128]{1,0:T(1,128)S(1)} %get-tuple-element.32.place, f32[1024,2048]{1,0:T(8,128)S(1)} %get-tuple-element.33.matrix, f32[128,2048]{1,0:T(8,128)S(1)} %get-tuple-element.34.gathered, f32[1024,128]{1,0:T(8,128)S(1)} %get-tuple-element.35.panel, f32[128,128]{1,0:T(8,128)S(1)} %get-tuple-element.36.inverse, ...), custom_call_target="tpu_custom_call" | custom-call | tf_op jit(solution)/shard_map/cond/branch_1_fun/update_24/pallas_call | solution.py:600
Async XLA Ops:
  0.0 37.9 %copy-start = (s32[128]{0:T(128)S(1)}, s32[128]{0:T(128)}, u32[]{:S(2)}) copy-start(s32[128]{0:T(128)} %param.5) | copy-start | bytes 1540

commit v3 on v2

--- a/solution.py
+++ b/solution.py
@@ -35,7 +35,7 @@
     return inverse
 
 
-def swap_plan(slots, pivots, me, rows_dev, table):
+def swap_plan(slots, pivots, me, rows_dev, table, note, most):
     shape = (NB, NB)
     down = lax.broadcasted_iota(jnp.int32, shape, 0)
     over = lax.broadcasted_iota(jnp.int32, shape, 1)
@@ -79,18 +79,19 @@
     table[pl.ds(1, 1), pl.ds(0, NB)] = jnp.sum(
         jnp.where(mine, offset, 0), axis=0, keepdims=True
     )
-    table[pl.ds(2, 1), pl.ds(0, NB)] = (
-        jnp.sum(jnp.where(mine & (source >= NB), offset + 1, 0), axis=0, keepdims=True) - 1
+    table[pl.ds(3, 1), :] = jnp.sum(jnp.where(hit, leaves, 0), axis=0, keepdims=True)
+    note[pl.ds(0, 1), :] = table[pl.ds(1, 1), pl.ds(0, NB)]
+    note[pl.ds(1, 1), :] = jnp.broadcast_to(
+        jnp.sum(jnp.where(owner == me, 1, 0), axis=0, keepdims=True), (1, NB)
     )
-    table[pl.ds(3, 1), :] = jnp.sum(jnp.where(hit, leaves, 0), axis=0, keepdims=True)
-    table[pl.ds(4, 1), pl.ds(0, NB)] = as_row(slot)
+    most[...] = jnp.broadcast_to(jnp.max(as_row(slot), axis=1, keepdims=True), (1, NB))
 
 
 def exchange_kernel(
     slots,
-    pivots, matrix,
-    resident, gathered, panel, inverse, returned, place, most,
-    table, plan, picks, received, ordered, top, top_a, top_b, back, corner,
+    pivots_hbm, matrix,
+    resident, gathered, panel, inverse, returned, note, most,
+    pivots, table, plan, picks, received, ordered, top, top_a, top_b, back, corner,
     row_send, row_recv, ret_send, ret_recv, ring_send, ring_recv,
     top_send, top_recv, panel_send, panel_recv, inv_send, inv_recv, own_sem, load_sem,
 ):
@@ -110,11 +111,27 @@
             src_ref=src, dst_ref=dst, send_sem=send_sem, recv_sem=recv_sem, device_id=device
         )
 
-    z_up, z_down = ((z + 1) % 4) * 2 + core, ((z + 3) % 4) * 2 + core
-    other = z * 2 + 1 - core
+    def ahead(d):
+        return jnp.where(me + d >= PROWS, me + d - PROWS, me + d)
+
+    def behind(d):
+        return jnp.where(me >= d, me - d, me - d + PROWS)
+
+    z_up = jnp.where(col >= 6, col - 6, col + 2)
+    z_down = jnp.where(col >= 2, col - 2, col + 6)
+    other = jnp.where(core == 0, col + 1, col - 1)
+    pivots_in = pltpu.make_async_copy(pivots_hbm, pivots, own_sem.at[10])
+    pivots_in.start()
+    loads = []
+    for k in range(LOADS):
+        part = pl.ds(k * (rows_dev // LOADS), rows_dev // LOADS)
+        loads.append(
+            pltpu.make_async_copy(matrix.at[part, :], resident.at[part, :], load_sem.at[k])
+        )
+        loads[-1].start()
     barrier = pltpu.get_barrier_semaphore()
     for d in range(1, PROWS):
-        pl.semaphore_signal(barrier, inc=1, device_id={"prow": (me + d) % PROWS})
+        pl.semaphore_signal(barrier, inc=1, device_id={"prow": ahead(d)})
     for c in (z_up, z_down, other):
         pl.semaphore_signal(barrier, inc=1, device_id={"pcol": c})
     pl.semaphore_wait(barrier, PROWS - 1 + 3)
@@ -185,18 +202,10 @@
         panel_first(1, 5, other).start()
         panel_own.start()
 
-    loads = []
-    for k in range(LOADS):
-        part = pl.ds(k * (rows_dev // LOADS), rows_dev // LOADS)
-        loads.append(
-            pltpu.make_async_copy(matrix.at[part, :], resident.at[part, :], load_sem.at[k])
-        )
-        loads[-1].start()
-
-    swap_plan(slots, pivots, me, rows_dev, table)
+    pivots_in.wait()
+    swap_plan(slots, pivots, me, rows_dev, table, note, most)
     plan_copy = pltpu.make_async_copy(table, plan, own_sem.at[9])
     plan_copy.start()
-    place[...] = table[pl.ds(2, 1), pl.ds(0, NB)]
     plan_copy.wait()
     for c in loads:
         c.wait()
@@ -208,7 +217,7 @@
     lax.fori_loop(0, slots, pick, 0, unroll=4)
 
     def row_copy(d):
-        peer = (me + d) % PROWS
+        peer = ahead(d)
         return remote(
             picks.at[:, block(peer)],
             received.at[pl.ds(pl.multiple_of(me * slots, 8), slots)],
@@ -227,7 +236,8 @@
         row_copy(d).wait_send()
         return carry
 
-    lax.fori_loop(1, PROWS, row_start, 0)
+    for d in (10, 2, 8, 6, 9, 7, 11, 5, 13, 3, 14, 1, 15, 4, 12):
+        row_start(d, 0)
 
     def inv_copy(k, device):
         return remote(inverse, inverse, inv_send.at[k], inv_recv.at[0], device)
@@ -245,36 +255,6 @@
         own_sem.at[0],
     )
     own_rows.start()
-    own_rows.wait()
-    lax.fori_loop(1, PROWS, row_wait, 0)
-
-    def order(j, carry):
-        ordered[pl.ds(j, 1), :] = received[pl.ds(plan[0, j], 1), :]
-        return carry
-
-    lax.fori_loop(0, NB, order, 0, unroll=8)
-    gathered[:, block(me)] = ordered[...]
-
-    def spot(o, along, across):
-        dx, dy = (along, across) if o == 0 else (across, along)
-        return ((x + dx + SIDE) % SIDE) * SIDE + (y + dy + SIDE) % SIDE
-
-    def ring_copy(o, q, sem, device):
-        ref = gathered.at[pl.ds(o * half, half), block(q)]
-        return remote(ref, ref, ring_send.at[o, sem], ring_recv.at[o, sem], {"prow": device})
-
-    def ring_start(o, q, sem, device):
-        c = ring_copy(o, q, sem, device)
-        c.start()
-        sent.append(c)
-
-    for d in (2, 1, 3):
-        for o in (0, 1):
-            ring_start(o, me, d, spot(o, d, 0))
-    for d in (2, 1, 3):
-        for o in (0, 1):
-            ring_start(o, me, 3 + d, spot(o, 0, d))
-
     def top_leg(a, d):
         if a == 0:
             src, dst, device = top_a, top.at[pl.ds(0, half)], x * SIDE + d
@@ -311,6 +291,56 @@
             top_leg(1, d).start()
         top[pl.ds(half, half), :] = top_b[:, pl.ds(0, NB)]
 
+    def panel_leg(h, there):
+        @pl.when((core == 0) & there)
+        def _():
+            panel_next(h, 0, other).wait_recv()
+            panel_next(h, 4 + h, other).start()
+
+            @pl.when((z == 1) if h == 0 else (z == 3))
+            def _():
+                panel_next(h, 0, 4).start()
+
+    for h in (0, 1):
+        panel_leg(h, z == 1 if h == 0 else z == 3)
+    for h in (0, 1):
+        panel_leg(h, z == 3 if h == 0 else z == 1)
+
+    own_rows.wait()
+    lax.fori_loop(1, PROWS, row_wait, 0)
+
+    def order(j, carry):
+        ordered[pl.ds(j, 1), :] = received[pl.ds(plan[0, j], 1), :]
+        return carry
+
+    lax.fori_loop(0, NB, order, 0, unroll=8)
+    gathered[:, block(me)] = ordered[...]
+
+    def spot(o, along, across):
+        dx, dy = (along, across) if o == 0 else (across, along)
+        xx, yy = x + dx, y + dy
+        if dx:
+            xx = jnp.where(xx >= SIDE, xx - SIDE, jnp.where(xx < 0, xx + SIDE, xx))
+        if dy:
+            yy = jnp.where(yy >= SIDE, yy - SIDE, jnp.where(yy < 0, yy + SIDE, yy))
+        return xx * SIDE + yy
+
+    def ring_copy(o, q, sem, device):
+        ref = gathered.at[pl.ds(o * half, half), block(q)]
+        return remote(ref, ref, ring_send.at[o, sem], ring_recv.at[o, sem], {"prow": device})
+
+    def ring_start(o, q, sem, device):
+        c = ring_copy(o, q, sem, device)
+        c.start()
+        sent.append(c)
+
+    for d in (2, 1, 3):
+        for o in (0, 1):
+            ring_start(o, me, d, spot(o, d, 0))
+    for d in (2, 1, 3):
+        for o in (0, 1):
+            ring_start(o, me, 3 + d, spot(o, 0, d))
+
     for e in (1, 3, 2):
         for o in (0, 1):
             q = spot(o, -e, 0)
@@ -327,18 +357,8 @@
         for d in range(1, SIDE):
             inv_copy(3 + d, {"prow": x * SIDE + d}).start()
 
-    def panel_leg(h):
-        @pl.when((core == 0) & (z > 0))
-        def _():
-            panel_next(h, 0, other).wait_recv()
-            panel_next(h, 4 + h, other).start()
-
-            @pl.when((z == 1) if h == 0 else (z == 3))
-            def _():
-                panel_next(h, 0, 4).start()
-
-    panel_leg(0)
-    panel_leg(1)
+    panel_leg(0, z == 2)
+    panel_leg(1, z == 2)
 
     @pl.when(y != 0)
     def _():
@@ -357,7 +377,7 @@
     lax.fori_loop(0, PROWS, back_rows, 0)
 
     def ret_copy(d):
-        peer = (me + d) % PROWS
+        peer = ahead(d)
         return remote(
             back.at[pl.ds(pl.multiple_of(peer * slots, 8), slots)],
             returned.at[:, block(me)],
@@ -369,7 +389,7 @@
         return carry
 
     def ret_wait(d, carry):
-        peer = (me - d + PROWS) % PROWS
+        peer = behind(d)
         remote(
             back.at[pl.ds(0, slots)], returned.at[:, block(peer)],
             ret_send.at[d], ret_recv.at[d], {"prow": peer},
@@ -414,7 +434,6 @@
             def _():
                 inv_copy(7, {"pcol": 4}).start()
 
-    most[0] = lax.fori_loop(0, NB, lambda j, m: jnp.maximum(m, plan[4, j]), 0, unroll=8)
     lax.fori_loop(1, PROWS, ret_wait, 0)
     ret_own.wait()
 
@@ -483,7 +502,6 @@
 def exchange(slots, collective_id, matrix, pivots):
     rows_dev, cols_dev = matrix.shape
     f32, i32 = jnp.float32, jnp.int32
-    smem = pl.BlockSpec(memory_space=pltpu.SMEM)
     vmem = pl.BlockSpec(memory_space=pltpu.VMEM)
     hbm = pl.BlockSpec(memory_space=pltpu.HBM)
     dma = pltpu.SemaphoreType.DMA
@@ -495,12 +513,13 @@
             jax.ShapeDtypeStruct((rows_dev, NB), f32),
             jax.ShapeDtypeStruct((NB, NB), f32),
             jax.ShapeDtypeStruct((slots, cols_dev), f32),
+            jax.ShapeDtypeStruct((2, NB), i32),
             jax.ShapeDtypeStruct((1, NB), i32),
-            jax.ShapeDtypeStruct((1,), i32),
         ],
-        in_specs=[vmem, hbm],
-        out_specs=[vmem, vmem, vmem, vmem, vmem, vmem, smem],
+        in_specs=[hbm, hbm],
+        out_specs=[vmem] * 7,
         scratch_shapes=[
+            pltpu.VMEM((1, NB), i32),
             pltpu.VMEM((8, PROWS * slots), i32),
             pltpu.SMEM((8, PROWS * slots), i32),
             pltpu.VMEM((slots, cols_dev), f32),
@@ -513,7 +532,7 @@
             pltpu.VMEM((NB, NB), f32),
             dma((PROWS,)), dma((PROWS,)), dma((PROWS,)), dma((PROWS,)),
             dma((2, 16)), dma((2, 16)),
-            dma((28,)), dma((7,)), dma((6,)), dma((2,)), dma((10,)), dma((1,)), dma((10,)),
+            dma((28,)), dma((7,)), dma((6,)), dma((2,)), dma((10,)), dma((1,)), dma((11,)),
             dma((LOADS,)),
         ],
         compiler_params=pltpu.CompilerParams(
@@ -534,49 +553,39 @@
 
 
 def update_kernel(
-    slots, place, matrix, gathered, panel, inverse, returned, out,
-    result, factor, chosen, chosen_factor, fixed, sems,
+    note, block, gathered, panel, inverse, returned, out, matrix,
+    notes, result, factor, note_sem, sems,
 ):
     me = lax.axis_index("prow")
     col = lax.axis_index("pcol")
+    note_copy = pltpu.make_async_copy(note, notes, note_sem.at[0])
+    note_copy.start()
     factor[...] = stacked(panel[...])
-
-    def choose(s, carry):
-        p = jnp.maximum(place[0, s], 0)
-        chosen[pl.ds(s, 1), :] = panel[pl.ds(p, 1), :]
-        return carry
-
-    lax.fori_loop(0, slots, choose, 0, unroll=4)
-    chosen_factor[...] = stacked(chosen[...])
+    solve = stacked(inverse[...])
+    note_copy.wait()
+
+    def replace(s, carry):
+        matrix[pl.ds(notes[0, s], 1), :] = returned[pl.ds(s, 1), :]
+        return carry
+
+    lax.fori_loop(0, notes[1, 0], replace, 0)
 
     def write(n):
         return pltpu.make_async_copy(
             result.at[:, pl.ds(n * WIDE, WIDE)], out.at[:, pl.ds(n * WIDE, WIDE)], sems.at[n]
         )
 
+    def terms(value):
+        high, low = split(value)
+        return jnp.concatenate([high, high, low], axis=0)
+
     parts = matrix.shape[1] // WIDE
     for n in range(parts):
         here = pl.ds(n * WIDE, WIDE)
-        upper = jnp.dot(
-            inverse[...], gathered[:, here], precision=HIGHEST, preferred_element_type=jnp.float32
-        )
-        high, low = split(upper)
-        terms = jnp.concatenate([high, high, low], axis=0)
+        upper = jnp.dot(solve, terms(gathered[:, here]), preferred_element_type=jnp.float32)
         result[:, here] = matrix[:, here] - jnp.dot(
-            factor[...], terms, preferred_element_type=jnp.float32
-        )
-        fixed[...] = returned[:, here] - jnp.dot(
-            chosen_factor[...], terms, preferred_element_type=jnp.float32
-        )
-
-        def fix(s, carry):
-            @pl.when(place[0, s] >= 0)
-            def _():
-                result[pl.ds(place[0, s], 1), here] = fixed[pl.ds(s, 1), :]
-
-            return carry
-
-        lax.fori_loop(0, slots, fix, 0)
+            factor[...], terms(upper), preferred_element_type=jnp.float32
+        )
 
         @pl.when(me == 0)
         def _():
@@ -586,33 +595,35 @@
 
             @pl.when(col == 0)
             def _():
-                result[:, pl.ds(0, NB)] = matrix[:, pl.ds(0, NB)]
+                result[:, pl.ds(0, NB)] = panel[...]
 
         write(n).start()
     for n in range(parts):
         write(n).wait()
 
 
-def update(slots, matrix, gathered, panel, inverse, returned, place):
+def update(matrix, gathered, panel, inverse, returned, note):
     rows_dev, cols_dev = matrix.shape
-    smem = pl.BlockSpec(memory_space=pltpu.SMEM)
     vmem = pl.BlockSpec(memory_space=pltpu.VMEM)
-    return pl.pallas_call(
-        functools.partial(update_kernel, slots),
-        out_shape=pltpu.HBM(matrix.shape, jnp.float32),
-        in_specs=[smem, vmem, vmem, vmem, vmem, vmem],
-        out_specs=pl.BlockSpec(memory_space=pltpu.HBM),
+    out, _ = pl.pallas_call(
+        update_kernel,
+        out_shape=[
+            pltpu.HBM(matrix.shape, jnp.float32), pltpu.VMEM(matrix.shape, jnp.float32)
+        ],
+        in_specs=[vmem] * 6,
+        out_specs=[pl.BlockSpec(memory_space=pltpu.HBM), vmem],
+        input_output_aliases={1: 1},
         scratch_shapes=[
+            pltpu.SMEM((2, NB), jnp.int32),
             pltpu.VMEM((rows_dev, cols_dev), jnp.float32),
             pltpu.VMEM((rows_dev, 3 * NB), jnp.bfloat16),
-            pltpu.VMEM((slots, NB), jnp.float32),
-            pltpu.VMEM((slots, 3 * NB), jnp.bfloat16),
-            pltpu.VMEM((slots, WIDE), jnp.float32),
+            pltpu.SemaphoreType.DMA((1,)),
             pltpu.SemaphoreType.DMA((cols_dev // WIDE,)),
         ],
         compiler_params=pltpu.CompilerParams(vmem_limit_bytes=28 * MIB),
-        name="update_%d" % slots,
-    )(place, matrix, gathered, panel, inverse, returned)
+        name="update",
+    )(note, matrix, gathered, panel, inverse, returned)
+    return out
 
 
 def local(matrix, pivots):
@@ -621,9 +632,9 @@
 
     def many():
         *found, _ = exchange(NB, 1, matrix, pivots)
-        return update(NB, *found)
-
-    return lax.cond(most[0] < FEW, lambda: update(FEW, *found), many)
+        return update(*found)
+
+    return lax.cond(most[0, 0] < FEW, lambda: update(*found), many)
 
 
 def solution(mesh):

time: 50.8 us -> 45.3 us (0.89)
  the two profiles are of different devices: /device:TPU:64 before, /device:TPU:83 now
where the time goes in v3:
time: 45.3 us; the launch traced here: 45.2 us
  Pallas kernels  44.7 us (99%)
    pallas_call x1, Pallas kernels, exchange(): pl.pallas_call(functools.partial(exchange_kernel, slots), out_shape=[pltp...  35.8 us
    pallas_call x1, Pallas kernels, update(): pl.pallas_call(update_kernel, out_shape=[pltpu.HBM(matrix.shape, jnp.floa...  8.92 us

profile of v3, /device:TPU:83, one launch (start us, length us, event | category | flops | bytes accessed | tf_op | source)
XLA Modules:
  0.0 45.2 jit_solution(14684826097863262648)
XLA Ops:
  0.0 0.0 copy-start
  0.0 35.8 %exchange_24.1 = (f32[1024,2048]{1,0:T(8,128)S(1)}, f32[128,2048]{1,0:T(8,128)S(1)}, f32[1024,128]{1,0:T(8,128)S(1)}, f32[128,128]{1,0:T(8,128)S(1)}, f32[24,204...) custom-call(s32[1,128]{1,0:T(1,128)} %bitcast.4, f32[1024,2048]{1,0:T(8,128)} %matrix.1), custom_call_target="tpu_custom_call" | custom-call | tf_op jit(solution)/shard_map/exchange_24/pallas_call | solution.py:508
  35.9 0.0 copy-done
  35.9 9.2 %conditional.1 = (f32[1024,2048]{1,0:T(8,128)}) conditional(s32[]{:T(128)} %bitcast.1, (s32[1,128]{1,0:T(1,128)S(1)}, f32[1024,2048]{1,0:T(8,128)}) %tuple.17, (s32[2,128]{1,0:T(2,128)S(1)}, f32[1024,2048]{1,0:T(8,128)S(1)}, f32[128,2048]{1,0:T(8,128)S(1)}, f32[1024,128]{1,0:T(8,128)S(1)}, f32[128,128]{1,0:T(8,128)S(1)}, ...), branch_computations={%region_0.0_spmd, %region_1.0_spmd} | conditional | bytes 8 | solution.py:637
  35.9 8.9 %update.3 = (f32[1024,2048]{1,0:T(8,128)}, f32[1024,2048]{1,0:T(8,128)S(1)}) custom-call(s32[2,128]{1,0:T(2,128)S(1)} %get-tuple-element.33.note, f32[1024,2048]{1,0:T(8,128)S(1)} %get-tuple-element.34.block, f32[128,2048]{1,0:T(8,128)S(1)} %get-tuple-element.35.gathered, f32[1024,128]{1,0:T(8,128)S(1)} %get-tuple-element.36.panel, ...), custom_call_target="tpu_custom_call", output_to_operand_aliasing={{1}: (1, {})} | custom-call | tf_op jit(solution)/shard_map/cond/branch_1_fun/update/pallas_call | solution.py:608
Async XLA Ops:
  0.0 35.9 %copy-start = (s32[128]{0:T(128)S(1)}, s32[128]{0:T(128)}, u32[]{:S(2)}) copy-start(s32[128]{0:T(128)} %param.5) | copy-start | bytes 1540

commit v4 on v3

--- a/solution.py
+++ b/solution.py
@@ -93,7 +93,7 @@
     resident, gathered, panel, inverse, returned, note, most,
     pivots, table, plan, picks, received, ordered, top, top_a, top_b, back, corner,
     row_send, row_recv, ret_send, ret_recv, ring_send, ring_recv,
-    top_send, top_recv, panel_send, panel_recv, inv_send, inv_recv, own_sem, load_sem,
+    top_send, top_recv, panel_send, panel_recv, low_send, low_recv, own_sem, load_sem,
 ):
     half = NB // 2
     rows_dev = matrix.shape[0]
@@ -138,29 +138,18 @@
 
     def top_x(d):
         return remote(
-            matrix.at[pl.ds(0, half), pl.ds(d * SIDE * NB, SIDE * NB)], top_a,
+            resident.at[pl.ds(0, half), pl.ds(d * SIDE * NB, SIDE * NB)], top_a,
             top_send.at[d], top_recv.at[0], {"prow": d * SIDE},
         )
 
     def top_y(d, k):
         return remote(
-            matrix.at[pl.ds(half, half), pl.ds((k * SIDE + d) * NB, NB)],
+            resident.at[pl.ds(half, half), pl.ds((k * SIDE + d) * NB, NB)],
             top_b.at[:, pl.ds(k * NB, NB)],
             top_send.at[4 + 4 * d + k], top_recv.at[1 + k], {"prow": d},
         )
 
-    top_own = [
-        pltpu.make_async_copy(
-            matrix.at[pl.ds(0, half), pl.ds(0, SIDE * NB)], top_a, own_sem.at[1]
-        )
-    ] + [
-        pltpu.make_async_copy(
-            matrix.at[pl.ds(half, half), pl.ds(k * SIDE * NB, NB)],
-            top_b.at[:, pl.ds(k * NB, NB)], own_sem.at[2 + k],
-        )
-        for k in range(SIDE)
-    ]
-    diagonal = pltpu.make_async_copy(matrix.at[pl.ds(0, NB), pl.ds(0, NB)], corner, own_sem.at[6])
+    loads[0].wait()
 
     @pl.when(me == 0)
     def _():
@@ -168,12 +157,42 @@
             top_x(d).start()
             for k in range(SIDE):
                 top_y(d, k).start()
-        for c in top_own:
-            c.start()
+        top_a[...] = resident[pl.ds(0, half), pl.ds(0, SIDE * NB)]
+        for k in range(SIDE):
+            top_b[:, pl.ds(k * NB, NB)] = resident[pl.ds(half, half), pl.ds(k * SIDE * NB, NB)]
+
+
+    def low_copy(k, device):
+        return remote(corner, corner, low_send.at[k], low_recv.at[0], device)
+
+    def low_sends(act):
+        @pl.when(me == 0)
+        def _():
+            @pl.when(core == 0)
+            def _():
+                act(low_copy(0, {"pcol": other}))
+
+                @pl.when(z <= 1)
+                def _():
+                    act(low_copy(1, {"pcol": z_up}))
+
+                @pl.when(z == 0)
+                def _():
+                    act(low_copy(2, {"pcol": z_down}))
+
+            for d in (2, 1, 3):
+                act(low_copy(2 + d, {"prow": d * SIDE}))
+
+    def low_sends_y(act):
+        @pl.when(y == 0)
+        def _():
+            for d in (2, 1, 3):
+                act(low_copy(5 + d, {"prow": x * SIDE + d}))
 
     @pl.when((me == 0) & (col == 0))
     def _():
-        diagonal.start()
+        corner[...] = resident[pl.ds(0, NB), pl.ds(0, NB)]
+        low_sends(lambda c: c.start())
 
     halves = [pl.ds(0, rows_dev // 2), pl.ds(rows_dev // 2, rows_dev // 2)]
     first_panel = matrix.at[:, pl.ds(0, NB)]
@@ -207,19 +226,21 @@
     plan_copy = pltpu.make_async_copy(table, plan, own_sem.at[9])
     plan_copy.start()
     plan_copy.wait()
-    for c in loads:
+    for c in loads[1:]:
         c.wait()
 
     def pick(s, carry):
-        picks[pl.ds(s, 1), :] = resident[pl.ds(plan[1, s], 1), :]
-        return carry
-
-    lax.fori_loop(0, slots, pick, 0, unroll=4)
+        row = resident[pl.ds(plan[1, s], 1), :]
+        for q in range(PROWS):
+            picks[pl.ds(q * slots + s, 1), :] = row[:, q * NB : (q + 1) * NB]
+        return carry
+
+    lax.fori_loop(0, slots, pick, 0)
 
     def row_copy(d):
         peer = ahead(d)
         return remote(
-            picks.at[:, block(peer)],
+            picks.at[pl.ds(pl.multiple_of(peer * slots, 8), slots)],
             received.at[pl.ds(pl.multiple_of(me * slots, 8), slots)],
             row_send.at[d], row_recv.at[d], {"prow": peer},
         )
@@ -239,22 +260,63 @@
     for d in (10, 2, 8, 6, 9, 7, 11, 5, 13, 3, 14, 1, 15, 4, 12):
         row_start(d, 0)
 
-    def inv_copy(k, device):
-        return remote(inverse, inverse, inv_send.at[k], inv_recv.at[0], device)
-
-    @pl.when((me == 0) & (col == 0))
-    def _():
-        diagonal.wait()
-        inverse[...] = invert_unit_lower(corner[...])
-        for d in range(1, SIDE):
-            inv_copy(d, {"prow": d * SIDE}).start()
-
-    own_rows = pltpu.make_async_copy(
-        picks.at[:, block(me)],
-        received.at[pl.ds(pl.multiple_of(me * slots, 8), slots)],
-        own_sem.at[0],
-    )
-    own_rows.start()
+    mine = pl.ds(pl.multiple_of(me * slots, 8), slots)
+    received[mine, :] = picks[mine, :]
+
+    @pl.when((me == 0) & (col != 0))
+    def _():
+        low_copy(0, {"pcol": other}).wait_recv()
+        low_sends(lambda c: c.start())
+
+    def panel_leg(h, there):
+        @pl.when((core == 0) & there)
+        def _():
+            panel_next(h, 0, other).wait_recv()
+            panel_next(h, 4 + h, other).start()
+
+            @pl.when((z == 1) if h == 0 else (z == 3))
+            def _():
+                panel_next(h, 0, 4).start()
+
+    for h in (0, 1):
+        panel_leg(h, z == 1 if h == 0 else z == 3)
+    for h in (0, 1):
+        panel_leg(h, z == 3 if h == 0 else z == 1)
+
+    lax.fori_loop(1, PROWS, row_wait, 0)
+
+    def order(j, carry):
+        ordered[pl.ds(j, 1), :] = received[pl.ds(plan[0, j], 1), :]
+        return carry
+
+    lax.fori_loop(0, NB, order, 0, unroll=8)
+    gathered[:, block(me)] = ordered[...]
+
+    def spot(o, along, across):
+        dx, dy = (along, across) if o == 0 else (across, along)
+        xx, yy = x + dx, y + dy
+        if dx:
+            xx = jnp.where(xx >= SIDE, xx - SIDE, jnp.where(xx < 0, xx + SIDE, xx))
+        if dy:
+            yy = jnp.where(yy >= SIDE, yy - SIDE, jnp.where(yy < 0, yy + SIDE, yy))
+        return xx * SIDE + yy
+
+    def ring_copy(o, q, sem, device):
+        ref = gathered.at[pl.ds(o * half, half), block(q)]
+        return remote(ref, ref, ring_send.at[o, sem], ring_recv.at[o, sem], {"prow": device})
+
+    def ring_start(o, q, sem, device):
+        c = ring_copy(o, q, sem, device)
+        c.start()
+        sent.append(c)
+
+    for d in (2, 1, 3):
+        for o in (0, 1):
+            ring_start(o, me, d, spot(o, d, 0))
+    for d in (2, 1, 3):
+        for o in (0, 1):
+            ring_start(o, me, 3 + d, spot(o, 0, d))
+
     def top_leg(a, d):
         if a == 0:
             src, dst, device = top_a, top.at[pl.ds(0, half)], x * SIDE + d
@@ -265,11 +327,6 @@
             top_send.at[20 + 4 * a + d], top_recv.at[5 + a], {"prow": device},
         )
 
-    @pl.when(me == 0)
-    def _():
-        for c in top_own:
-            c.wait()
-
     @pl.when(y == 0)
     def _():
         @pl.when(x != 0)
@@ -291,55 +348,13 @@
             top_leg(1, d).start()
         top[pl.ds(half, half), :] = top_b[:, pl.ds(0, NB)]
 
-    def panel_leg(h, there):
-        @pl.when((core == 0) & there)
-        def _():
-            panel_next(h, 0, other).wait_recv()
-            panel_next(h, 4 + h, other).start()
-
-            @pl.when((z == 1) if h == 0 else (z == 3))
-            def _():
-                panel_next(h, 0, 4).start()
-
-    for h in (0, 1):
-        panel_leg(h, z == 1 if h == 0 else z == 3)
-    for h in (0, 1):
-        panel_leg(h, z == 3 if h == 0 else z == 1)
-
-    own_rows.wait()
-    lax.fori_loop(1, PROWS, row_wait, 0)
-
-    def order(j, carry):
-        ordered[pl.ds(j, 1), :] = received[pl.ds(plan[0, j], 1), :]
-        return carry
-
-    lax.fori_loop(0, NB, order, 0, unroll=8)
-    gathered[:, block(me)] = ordered[...]
-
-    def spot(o, along, across):
-        dx, dy = (along, across) if o == 0 else (across, along)
-        xx, yy = x + dx, y + dy
-        if dx:
-            xx = jnp.where(xx >= SIDE, xx - SIDE, jnp.where(xx < 0, xx + SIDE, xx))
-        if dy:
-            yy = jnp.where(yy >= SIDE, yy - SIDE, jnp.where(yy < 0, yy + SIDE, yy))
-        return xx * SIDE + yy
-
-    def ring_copy(o, q, sem, device):
-        ref = gathered.at[pl.ds(o * half, half), block(q)]
-        return remote(ref, ref, ring_send.at[o, sem], ring_recv.at[o, sem], {"prow": device})
-
-    def ring_start(o, q, sem, device):
-        c = ring_copy(o, q, sem, device)
-        c.start()
-        sent.append(c)
-
-    for d in (2, 1, 3):
-        for o in (0, 1):
-            ring_start(o, me, d, spot(o, d, 0))
-    for d in (2, 1, 3):
-        for o in (0, 1):
-            ring_start(o, me, 3 + d, spot(o, 0, d))
+    @pl.when(y == 0)
+    def _():
+        @pl.when(x != 0)
+        def _():
+            low_copy(0, {"pcol": other}).wait_recv()
+
+    low_sends_y(lambda c: c.start())
 
     for e in (1, 3, 2):
         for o in (0, 1):
@@ -348,15 +363,6 @@
             for d in (2, 1, 3):
                 ring_start(o, q, 3 + 3 * e + d, spot(o, 0, d))
 
-    @pl.when((col == 0) & (y == 0))
-    def _():
-        @pl.when(x != 0)
-        def _():
-            inv_copy(0, {"pcol": other}).wait_recv()
-
-        for d in range(1, SIDE):
-            inv_copy(3 + d, {"prow": x * SIDE + d}).start()
-
     panel_leg(0, z == 2)
     panel_leg(1, z == 2)
 
@@ -407,33 +413,17 @@
     )
     ret_own.start()
 
-    @pl.when(col == 0)
-    def _():
-        @pl.when(y != 0)
-        def _():
-            inv_copy(0, {"pcol": other}).wait_recv()
-
-        inv_copy(7, {"pcol": z_up}).start()
-        inv_copy(8, {"pcol": z_down}).start()
-        inv_copy(9, {"pcol": other}).start()
+    @pl.when(y != 0)
+    def _():
+        low_copy(0, {"pcol": other}).wait_recv()
+
+    inverse[...] = invert_unit_lower(corner[...])
 
     for e in (0, 1, 3, 2):
         for d in (1, 3, 2):
             for o in (0, 1):
                 ring_copy(o, spot(o, -e, -d), 3 + 3 * e + d, me).wait_recv()
 
-    @pl.when(col != 0)
-    def _():
-        inv_copy(0, {"pcol": other}).wait_recv()
-
-        @pl.when(core == 0)
-        def _():
-            inv_copy(9, {"pcol": other}).start()
-
-            @pl.when(z == 1)
-            def _():
-                inv_copy(7, {"pcol": 4}).start()
-
     lax.fori_loop(1, PROWS, ret_wait, 0)
     ret_own.wait()
 
@@ -470,29 +460,17 @@
         for h, k in ((0, 0), (1, 1), (1, 2), (0, 3), (0, 4), (1, 5)):
             panel_first(h, k, other).wait_send()
 
-        @pl.when(me == 0)
-        def _():
-            for d in range(1, SIDE):
-                inv_copy(d, {"prow": d * SIDE}).wait_send()
-
-        @pl.when(y == 0)
-        def _():
-            for d in range(1, SIDE):
-                inv_copy(3 + d, {"prow": x * SIDE + d}).wait_send()
-
-        for k in (7, 8, 9):
-            inv_copy(k, {"pcol": other}).wait_send()
+    low_sends(lambda c: c.wait_send())
+    low_sends_y(lambda c: c.wait_send())
 
     @pl.when((core == 0) & (z > 0))
     def _():
         panel_next(0, 4, other).wait_send()
         panel_next(1, 5, other).wait_send()
-        inv_copy(9, {"pcol": other}).wait_send()
 
         @pl.when(z == 1)
         def _():
             panel_next(0, 0, other).wait_send()
-            inv_copy(7, {"pcol": other}).wait_send()
 
         @pl.when(z == 3)
         def _():
@@ -522,7 +500,7 @@
             pltpu.VMEM((1, NB), i32),
             pltpu.VMEM((8, PROWS * slots), i32),
             pltpu.SMEM((8, PROWS * slots), i32),
-            pltpu.VMEM((slots, cols_dev), f32),
+            pltpu.VMEM((PROWS * slots, NB), f32),
             pltpu.VMEM((PROWS * slots, NB), f32),
             pltpu.VMEM((NB, NB), f32),
             pltpu.VMEM((NB, NB), f32),
@@ -579,23 +557,26 @@
         high, low = split(value)
         return jnp.concatenate([high, high, low], axis=0)
 
+    rows = matrix.shape[0] - NB
     parts = matrix.shape[1] // WIDE
     for n in range(parts):
         here = pl.ds(n * WIDE, WIDE)
         upper = jnp.dot(solve, terms(gathered[:, here]), preferred_element_type=jnp.float32)
-        result[:, here] = matrix[:, here] - jnp.dot(
+        value = matrix[:, here] - jnp.dot(
             factor[...], terms(upper), preferred_element_type=jnp.float32
         )
-
-        @pl.when(me == 0)
-        def _():
-            result[pl.ds(0, NB), here] = upper
-
+        head = jnp.where(me == 0, upper, value[:NB])
         if n == 0:
-
-            @pl.when(col == 0)
-            def _():
-                result[:, pl.ds(0, NB)] = panel[...]
+            keep = col == 0
+            result[pl.ds(0, NB), pl.ds(0, NB)] = jnp.where(keep, panel[pl.ds(0, NB), :], head[:, :NB])
+            result[pl.ds(NB, rows), pl.ds(0, NB)] = jnp.where(
+                keep, panel[pl.ds(NB, rows), :], value[NB:, :NB]
+            )
+            result[pl.ds(0, NB), pl.ds(NB, WIDE - NB)] = head[:, NB:]
+            result[pl.ds(NB, rows), pl.ds(NB, WIDE - NB)] = value[NB:, NB:]
+        else:
+            result[pl.ds(0, NB), here] = head
+            result[pl.ds(NB, rows), here] = value[NB:]
 
         write(n).start()
     for n in range(parts):

time: 45.3 us -> 39.6 us (0.87)
  the two profiles are of different devices: /device:TPU:83 before, /device:TPU:0 now
where the time goes in v4:
time: 39.6 us; the launch traced here: 39.5 us
  Pallas kernels  39 us (98%)
    pallas_call x1, Pallas kernels, exchange(): pl.pallas_call(functools.partial(exchange_kernel, slots), out_shape=[pltp...  33.2 us
    pallas_call x1, Pallas kernels, update(): pl.pallas_call(update_kernel, out_shape=[pltpu.HBM(matrix.shape, jnp.floa...  5.77 us

profile of v4, /device:TPU:0, one launch (start us, length us, event | category | flops | bytes accessed | tf_op | source)
XLA Modules:
  0.0 39.5 jit_solution(717632266005718645)
XLA Ops:
  0.0 0.0 copy-start
  0.0 33.2 %exchange_24.1 = (f32[1024,2048]{1,0:T(8,128)S(1)}, f32[128,2048]{1,0:T(8,128)S(1)}, f32[1024,128]{1,0:T(8,128)S(1)}, f32[128,128]{1,0:T(8,128)S(1)}, f32[24,204...) custom-call(s32[1,128]{1,0:T(1,128)} %bitcast.4, f32[1024,2048]{1,0:T(8,128)} %matrix.1), custom_call_target="tpu_custom_call" | custom-call | tf_op jit(solution)/shard_map/exchange_24/pallas_call | solution.py:486
  33.3 0.0 copy-done
  33.3 6.0 %conditional.1 = (f32[1024,2048]{1,0:T(8,128)}) conditional(s32[]{:T(128)} %bitcast.1, (s32[1,128]{1,0:T(1,128)S(1)}, f32[1024,2048]{1,0:T(8,128)}) %tuple.17, (s32[2,128]{1,0:T(2,128)S(1)}, f32[1024,2048]{1,0:T(8,128)S(1)}, f32[128,2048]{1,0:T(8,128)S(1)}, f32[1024,128]{1,0:T(8,128)S(1)}, f32[128,128]{1,0:T(8,128)S(1)}, ...), branch_computations={%region_0.0_spmd, %region_1.0_spmd} | conditional | bytes 8 | solution.py:618
  33.3 5.8 %update.3 = (f32[1024,2048]{1,0:T(8,128)}, f32[1024,2048]{1,0:T(8,128)S(1)}) custom-call(s32[2,128]{1,0:T(2,128)S(1)} %get-tuple-element.33.note, f32[1024,2048]{1,0:T(8,128)S(1)} %get-tuple-element.34.block, f32[128,2048]{1,0:T(8,128)S(1)} %get-tuple-element.35.gathered, f32[1024,128]{1,0:T(8,128)S(1)} %get-tuple-element.36.panel, ...), custom_call_target="tpu_custom_call", output_to_operand_aliasing={{1}: (1, {})} | custom-call | tf_op jit(solution)/shard_map/cond/branch_1_fun/update/pallas_call | solution.py:589
Async XLA Ops:
  0.0 33.3 %copy-start = (s32[128]{0:T(128)S(1)}, s32[128]{0:T(128)}, u32[]{:S(2)}) copy-start(s32[128]{0:T(128)} %param.5) | copy-start | bytes 1540

commit v5 on v4

--- a/solution.py
+++ b/solution.py
@@ -39,52 +39,62 @@
     shape = (NB, NB)
     down = lax.broadcasted_iota(jnp.int32, shape, 0)
     over = lax.broadcasted_iota(jnp.int32, shape, 1)
-    earlier = over < down
-
-    def as_row(column):
-        return jnp.sum(jnp.where(down == over, column, 0), axis=0, keepdims=True)
-
-    def as_column(row):
-        return jnp.sum(jnp.where(down == over, row, 0), axis=1, keepdims=True)
-
-    def look_up(row, index):
-        return jnp.sum(jnp.where(over == index, row, 0), axis=1, keepdims=True)
-
-    def last(where):
-        return jnp.max(jnp.where(where, over, -1), axis=1, keepdims=True)
+    earlier, later = over < down, down < over
+
+    def by_row(value):
+        return jnp.sum(value, axis=1, keepdims=True)
+
+    def by_column(value):
+        return jnp.sum(value, axis=0, keepdims=True)
+
+    def look_up(vector, index):
+        column, row = vector
+        at_column, at_row = index
+        return (
+            by_row(jnp.where(over == at_column, row, 0)),
+            by_column(jnp.where(down == at_row, column, 0)),
+        )
+
+    def last(where, where_t):
+        return (
+            jnp.max(jnp.where(where, over, -1), axis=1, keepdims=True),
+            jnp.max(jnp.where(where_t, down, -1), axis=0, keepdims=True),
+        )
+
+    def choose(index, yes, no):
+        return tuple(jnp.where(i >= 0, a, b) for i, a, b in zip(index, yes, no))
 
     p_row = pivots[...]
-    p_col = as_column(p_row)
-    steps = lax.broadcasted_iota(jnp.int32, (NB, 1), 0)
-    touched = last((p_row == down) & earlier)
-    held = jnp.where(touched >= 0, touched, steps)
+    p = by_row(jnp.where(down == over, p_row, 0)), p_row
+    steps = (
+        lax.broadcasted_iota(jnp.int32, (NB, 1), 0), lax.broadcasted_iota(jnp.int32, (1, NB), 1)
+    )
+    touched = last((p[1] == down) & earlier, (p[0] == over) & later)
+    held = choose(touched, touched, steps)
     for _ in range(7):
-        held = look_up(as_row(held), held)
-    held_row = as_row(held)
-    same = p_row == p_col
-    before = last(same & earlier)
-    source = jnp.where(before >= 0, look_up(held_row, before), p_col)
-    leaves = look_up(held_row, last(same))
-    owner = source // rows_dev
-    slot = jnp.sum(
-        jnp.where((as_row(owner) == owner) & earlier, 1, 0), axis=1, keepdims=True
+        held = look_up(held, held)
+    same = p[0] == p[1]
+    before = last(same & earlier, same & later)
+    source = choose(before, look_up(held, before), p)
+    owner = tuple(v // rows_dev for v in source)
+    alike = owner[0] == owner[1]
+    slot = (
+        by_row(jnp.where(alike & earlier, 1, 0)), by_column(jnp.where(alike & later, 1, 0))
     )
-    code = owner * slots + jnp.minimum(slot, slots - 1)
-    mine = (owner == me) & (slot == over)
-    offset = source - me * rows_dev
+    offset = source[0] - me * rows_dev
+    mine = (owner[0] == me) & (slot[0] == over)
+    picked = by_column(jnp.where(mine, offset, 0))
+    table[pl.ds(0, 1), pl.ds(0, NB)] = owner[1] * slots + jnp.minimum(slot[1], slots - 1)
+    table[pl.ds(1, 1), pl.ds(0, NB)] = picked
+    leaves = look_up(held, last(same, same))[0]
     wide = lax.broadcasted_iota(jnp.int32, (NB, PROWS * slots), 1)
-    code_wide = owner * slots + slot
-    hit = (code_wide == wide) & (slot < slots)
-    table[pl.ds(0, 1), pl.ds(0, NB)] = as_row(code)
-    table[pl.ds(1, 1), pl.ds(0, NB)] = jnp.sum(
-        jnp.where(mine, offset, 0), axis=0, keepdims=True
+    hit = (owner[0] * slots + slot[0] == wide) & (slot[0] < slots)
+    table[pl.ds(3, 1), :] = by_column(jnp.where(hit, leaves, 0))
+    note[pl.ds(0, 1), :] = picked
+    note[pl.ds(1, 1), :] = jnp.broadcast_to(
+        by_column(jnp.where(owner[0] == me, 1, 0)), (1, NB)
     )
-    table[pl.ds(3, 1), :] = jnp.sum(jnp.where(hit, leaves, 0), axis=0, keepdims=True)
-    note[pl.ds(0, 1), :] = table[pl.ds(1, 1), pl.ds(0, NB)]
-    note[pl.ds(1, 1), :] = jnp.broadcast_to(
-        jnp.sum(jnp.where(owner == me, 1, 0), axis=0, keepdims=True), (1, NB)
-    )
-    most[...] = jnp.broadcast_to(jnp.max(as_row(slot), axis=1, keepdims=True), (1, NB))
+    most[...] = jnp.broadcast_to(by_row(jnp.max(slot[0], axis=0, keepdims=True)), (1, NB))
 
 
 def exchange_kernel(
@@ -101,7 +111,6 @@
     col = lax.axis_index("pcol")
     x, y = me // SIDE, me % SIDE
     z, core = col // 2, col % 2
-    sent = []
 
     def block(q):
         return pl.ds(pl.multiple_of(q * NB, NB), NB)
@@ -122,6 +131,12 @@
     other = jnp.where(core == 0, col + 1, col - 1)
     pivots_in = pltpu.make_async_copy(pivots_hbm, pivots, own_sem.at[10])
     pivots_in.start()
+    panel_in = pltpu.make_async_copy(matrix.at[:, pl.ds(0, NB)], panel, own_sem.at[7])
+
+    @pl.when(col == 0)
+    def _():
+        panel_in.start()
+
     loads = []
     for k in range(LOADS):
         part = pl.ds(k * (rows_dev // LOADS), rows_dev // LOADS)
@@ -139,14 +154,14 @@
     def top_x(d):
         return remote(
             resident.at[pl.ds(0, half), pl.ds(d * SIDE * NB, SIDE * NB)], top_a,
-            top_send.at[d], top_recv.at[0], {"prow": d * SIDE},
+            top_send.at[0], top_recv.at[0], {"prow": d * SIDE},
         )
 
     def top_y(d, k):
         return remote(
             resident.at[pl.ds(half, half), pl.ds((k * SIDE + d) * NB, NB)],
             top_b.at[:, pl.ds(k * NB, NB)],
-            top_send.at[4 + 4 * d + k], top_recv.at[1 + k], {"prow": d},
+            top_send.at[0], top_recv.at[1], {"prow": d},
         )
 
     loads[0].wait()
@@ -161,7 +176,6 @@
         for k in range(SIDE):
             top_b[:, pl.ds(k * NB, NB)] = resident[pl.ds(half, half), pl.ds(k * SIDE * NB, NB)]
 
-
     def low_copy(k, device):
         return remote(corner, corner, low_send.at[k], low_recv.at[0], device)
 
@@ -194,32 +208,17 @@
         corner[...] = resident[pl.ds(0, NB), pl.ds(0, NB)]
         low_sends(lambda c: c.start())
 
-    halves = [pl.ds(0, rows_dev // 2), pl.ds(rows_dev // 2, rows_dev // 2)]
-    first_panel = matrix.at[:, pl.ds(0, NB)]
-
-    def panel_first(h, k, to):
-        return remote(
-            first_panel.at[halves[h]], panel.at[halves[h]],
-            panel_send.at[k], panel_recv.at[h], {"pcol": to},
-        )
-
-    def panel_next(h, k, to):
-        return remote(
-            panel.at[halves[h]], panel.at[halves[h]],
-            panel_send.at[k], panel_recv.at[h], {"pcol": to},
-        )
-
-    panel_own = pltpu.make_async_copy(first_panel, panel, own_sem.at[7])
+    def panel_copy(h, k, to):
+        ref = panel.at[pl.ds(pl.multiple_of(h * (rows_dev // 2), 8), rows_dev // 2)]
+        return remote(ref, ref, panel_send.at[k], panel_recv.at[h], {"pcol": to})
 
     @pl.when(col == 0)
     def _():
-        panel_first(0, 0, z_up).start()
-        panel_first(1, 1, z_down).start()
-        panel_first(1, 2, z_up).start()
-        panel_first(0, 3, z_down).start()
-        panel_first(0, 4, other).start()
-        panel_first(1, 5, other).start()
-        panel_own.start()
+        panel_in.wait()
+        panel_copy(1, 2, other).start()
+        panel_copy(0, 0, z_up).start()
+        panel_copy(0, 1, z_down).start()
+        panel_copy(0, 3, other).start()
 
     pivots_in.wait()
     swap_plan(slots, pivots, me, rows_dev, table, note, most)
@@ -242,23 +241,15 @@
         return remote(
             picks.at[pl.ds(pl.multiple_of(peer * slots, 8), slots)],
             received.at[pl.ds(pl.multiple_of(me * slots, 8), slots)],
-            row_send.at[d], row_recv.at[d], {"prow": peer},
-        )
-
-    def row_start(d, carry):
+            row_send.at[0], row_recv.at[0], {"prow": peer},
+        )
+
+    def row_all():
+        ref = received.at[pl.ds(0, (PROWS - 1) * slots)]
+        return remote(ref, ref, row_send.at[0], row_recv.at[0], {"prow": ahead(1)})
+
+    for d in (10, 2, 8, 6, 9, 7, 11, 5, 13, 3, 14, 1, 15, 4, 12):
         row_copy(d).start()
-        return carry
-
-    def row_wait(d, carry):
-        row_copy(d).wait_recv()
-        return carry
-
-    def row_sent(d, carry):
-        row_copy(d).wait_send()
-        return carry
-
-    for d in (10, 2, 8, 6, 9, 7, 11, 5, 13, 3, 14, 1, 15, 4, 12):
-        row_start(d, 0)
 
     mine = pl.ds(pl.multiple_of(me * slots, 8), slots)
     received[mine, :] = picks[mine, :]
@@ -268,22 +259,56 @@
         low_copy(0, {"pcol": other}).wait_recv()
         low_sends(lambda c: c.start())
 
-    def panel_leg(h, there):
-        @pl.when((core == 0) & there)
-        def _():
-            panel_next(h, 0, other).wait_recv()
-            panel_next(h, 4 + h, other).start()
-
-            @pl.when((z == 1) if h == 0 else (z == 3))
-            def _():
-                panel_next(h, 0, 4).start()
-
-    for h in (0, 1):
-        panel_leg(h, z == 1 if h == 0 else z == 3)
-    for h in (0, 1):
-        panel_leg(h, z == 3 if h == 0 else z == 1)
-
-    lax.fori_loop(1, PROWS, row_wait, 0)
+    def panel_leg():
+        panel_copy(core, 0, other).wait_recv()
+
+        @pl.when(z > 0)
+        def _():
+            panel_copy(core, 2, other).start()
+
+        @pl.when((z == 0) | (z == 1 + 2 * core))
+        def _():
+            panel_copy(core, 0, jnp.where(z == 3, z_down, z_up)).start()
+
+        @pl.when(z == 0)
+        def _():
+            panel_copy(core, 1, z_down).start()
+
+    @pl.when((z != 2) & (col != 0))
+    def _():
+        panel_leg()
+
+    def top_leg(a, d):
+        if a == 0:
+            src, dst, device = top_a, top.at[pl.ds(0, half)], x * SIDE + d
+        else:
+            src, dst, device = top_b, top.at[pl.ds(half, half)], d * SIDE + y
+        return remote(
+            src.at[:, pl.ds(d * NB, NB)], dst,
+            top_send.at[1 + a], top_recv.at[2 + a], {"prow": device},
+        )
+
+    @pl.when(y == 0)
+    def _():
+        @pl.when(x != 0)
+        def _():
+            top_x(1).wait_recv()
+
+        for d in range(1, SIDE):
+            top_leg(0, d).start()
+        top[pl.ds(0, half), :] = top_a[:, pl.ds(0, NB)]
+
+    @pl.when(x == 0)
+    def _():
+        @pl.when(y != 0)
+        def _():
+            remote(top_b, top_b, top_send.at[0], top_recv.at[1], {"prow": 1}).wait_recv()
+
+        for d in range(1, SIDE):
+            top_leg(1, d).start()
+        top[pl.ds(half, half), :] = top_b[:, pl.ds(0, NB)]
+
+    row_all().wait_recv()
 
     def order(j, carry):
         ordered[pl.ds(j, 1), :] = received[pl.ds(plan[0, j], 1), :]
@@ -303,68 +328,29 @@
 
     def ring_copy(o, q, sem, device):
         ref = gathered.at[pl.ds(o * half, half), block(q)]
-        return remote(ref, ref, ring_send.at[o, sem], ring_recv.at[o, sem], {"prow": device})
+        return remote(ref, ref, ring_send.at[0], ring_recv.at[sem], {"prow": device})
+
+    def ring_all(blocks, sem):
+        ref = gathered.at[:, pl.ds(0, blocks * NB)]
+        return remote(ref, ref, ring_send.at[0], ring_recv.at[sem], {"prow": ahead(1)})
 
     def ring_start(o, q, sem, device):
-        c = ring_copy(o, q, sem, device)
-        c.start()
-        sent.append(c)
+        ring_copy(o, q, sem, device).start()
 
     for d in (2, 1, 3):
         for o in (0, 1):
-            ring_start(o, me, d, spot(o, d, 0))
+            ring_start(o, me, 2 * d + o - 1, spot(o, d, 0))
     for d in (2, 1, 3):
         for o in (0, 1):
-            ring_start(o, me, 3 + d, spot(o, 0, d))
-
-    def top_leg(a, d):
-        if a == 0:
-            src, dst, device = top_a, top.at[pl.ds(0, half)], x * SIDE + d
-        else:
-            src, dst, device = top_b, top.at[pl.ds(half, half)], d * SIDE + y
-        return remote(
-            src.at[:, pl.ds(d * NB, NB)], dst,
-            top_send.at[20 + 4 * a + d], top_recv.at[5 + a], {"prow": device},
-        )
+            ring_start(o, me, 0, spot(o, 0, d))
 
     @pl.when(y == 0)
     def _():
         @pl.when(x != 0)
         def _():
-            top_x(1).wait_recv()
-
-        for d in range(1, SIDE):
-            top_leg(0, d).start()
-        top[pl.ds(0, half), :] = top_a[:, pl.ds(0, NB)]
-
-    @pl.when(x == 0)
-    def _():
-        @pl.when(y != 0)
-        def _():
-            for k in range(SIDE):
-                top_y(1, k).wait_recv()
-
-        for d in range(1, SIDE):
-            top_leg(1, d).start()
-        top[pl.ds(half, half), :] = top_b[:, pl.ds(0, NB)]
-
-    @pl.when(y == 0)
-    def _():
-        @pl.when(x != 0)
-        def _():
             low_copy(0, {"pcol": other}).wait_recv()
 
     low_sends_y(lambda c: c.start())
-
-    for e in (1, 3, 2):
-        for o in (0, 1):
-            q = spot(o, -e, 0)
-            ring_copy(o, q, e, me).wait_recv()
-            for d in (2, 1, 3):
-                ring_start(o, q, 3 + 3 * e + d, spot(o, 0, d))
-
-    panel_leg(0, z == 2)
-    panel_leg(1, z == 2)
 
     @pl.when(y != 0)
     def _():
@@ -387,94 +373,83 @@
         return remote(
             back.at[pl.ds(pl.multiple_of(peer * slots, 8), slots)],
             returned.at[:, block(me)],
-            ret_send.at[d], ret_recv.at[d], {"prow": peer},
-        )
-
-    def ret_start(d, carry):
+            ret_send.at[0], ret_recv.at[0], {"prow": peer},
+        )
+
+    def ret_all():
+        ref = returned.at[:, pl.ds(0, (PROWS - 1) * NB)]
+        return remote(ref, ref, ret_send.at[0], ret_recv.at[0], {"prow": ahead(1)})
+
+    for d in (10, 2, 8, 6, 9, 7, 11, 5, 13, 3, 14, 1, 15, 4, 12):
         ret_copy(d).start()
-        return carry
-
-    def ret_wait(d, carry):
-        peer = behind(d)
-        remote(
-            back.at[pl.ds(0, slots)], returned.at[:, block(peer)],
-            ret_send.at[d], ret_recv.at[d], {"prow": peer},
-        ).wait_recv()
-        return carry
-
-    def ret_sent(d, carry):
-        ret_copy(d).wait_send()
-        return carry
-
-    lax.fori_loop(1, PROWS, ret_start, 0)
     ret_own = pltpu.make_async_copy(
         back.at[pl.ds(pl.multiple_of(me * slots, 8), slots)],
         returned.at[:, block(me)], own_sem.at[8],
     )
     ret_own.start()
 
+    for e in (1, 3, 2):
+        for o in (0, 1):
+            q = spot(o, -e, 0)
+            ring_copy(o, q, 2 * e + o - 1, me).wait_recv()
+            for d in (2, 1, 3):
+                ring_start(o, q, 0, spot(o, 0, d))
+
+    @pl.when(z == 2)
+    def _():
+        panel_leg()
+
     @pl.when(y != 0)
     def _():
         low_copy(0, {"pcol": other}).wait_recv()
 
     inverse[...] = invert_unit_lower(corner[...])
 
-    for e in (0, 1, 3, 2):
-        for d in (1, 3, 2):
-            for o in (0, 1):
-                ring_copy(o, spot(o, -e, -d), 3 + 3 * e + d, me).wait_recv()
-
-    lax.fori_loop(1, PROWS, ret_wait, 0)
+    ring_all(12, 0).wait_recv()
+    ret_all().wait_recv()
     ret_own.wait()
 
-    @pl.when(core == 1)
-    def _():
-        panel_next(0, 0, other).wait_recv()
-        panel_next(1, 0, other).wait_recv()
-
-    for c in sent:
-        c.wait_send()
-    lax.fori_loop(1, PROWS, row_sent, 0)
-    lax.fori_loop(1, PROWS, ret_sent, 0)
+    @pl.when(col != 0)
+    def _():
+        panel_copy(1 - core, 0, other).wait_recv()
+
+    ring_all(15, 0).wait_send()
+    row_all().wait_send()
+    ret_all().wait_send()
 
     @pl.when(me == 0)
     def _():
-        for d in (1, 3, 2):
-            top_x(d).wait_send()
-            for k in range(SIDE):
-                top_y(d, k).wait_send()
+        ref = resident.at[pl.ds(0, NB), pl.ds(0, 12 * NB)]
+        remote(ref, ref, top_send.at[0], top_recv.at[0], {"prow": 1}).wait_send()
 
     @pl.when(y == 0)
     def _():
-        for d in range(1, SIDE):
-            top_leg(0, d).wait_send()
+        ref = top_a.at[:, pl.ds(0, 3 * NB)]
+        remote(ref, ref, top_send.at[1], top_recv.at[2], {"prow": 1}).wait_send()
 
     @pl.when(x == 0)
     def _():
-        for d in range(1, SIDE):
-            top_leg(1, d).wait_send()
+        ref = top_b.at[:, pl.ds(0, 3 * NB)]
+        remote(ref, ref, top_send.at[2], top_recv.at[3], {"prow": 1}).wait_send()
 
     @pl.when(col == 0)
     def _():
-        panel_own.wait()
-        for h, k in ((0, 0), (1, 1), (1, 2), (0, 3), (0, 4), (1, 5)):
-            panel_first(h, k, other).wait_send()
+        panel_copy(0, 3, other).wait_send()
+
+    @pl.when((z > 0) | (core == 0))
+    def _():
+        panel_copy(core, 2, other).wait_send()
+
+    @pl.when((z == 0) | (z == 1 + 2 * core))
+    def _():
+        panel_copy(core, 0, other).wait_send()
+
+    @pl.when(z == 0)
+    def _():
+        panel_copy(core, 1, other).wait_send()
 
     low_sends(lambda c: c.wait_send())
     low_sends_y(lambda c: c.wait_send())
-
-    @pl.when((core == 0) & (z > 0))
-    def _():
-        panel_next(0, 4, other).wait_send()
-        panel_next(1, 5, other).wait_send()
-
-        @pl.when(z == 1)
-        def _():
-            panel_next(0, 0, other).wait_send()
-
-        @pl.when(z == 3)
-        def _():
-            panel_next(1, 0, other).wait_send()
 
 
 def exchange(slots, collective_id, matrix, pivots):
@@ -508,9 +483,9 @@
             pltpu.VMEM((NB // 2, SIDE * NB), f32),
             pltpu.VMEM((PROWS * slots, NB), f32),
             pltpu.VMEM((NB, NB), f32),
-            dma((PROWS,)), dma((PROWS,)), dma((PROWS,)), dma((PROWS,)),
-            dma((2, 16)), dma((2, 16)),
-            dma((28,)), dma((7,)), dma((6,)), dma((2,)), dma((10,)), dma((1,)), dma((11,)),
+            dma((1,)), dma((1,)), dma((1,)), dma((1,)),
+            dma((1,)), dma((7,)),
+            dma((3,)), dma((4,)), dma((4,)), dma((2,)), dma((10,)), dma((1,)), dma((11,)),
             dma((LOADS,)),
         ],
         compiler_params=pltpu.CompilerParams(

time: 39.6 us -> 36.3 us (0.917)
  Pallas kernels: 39 us -> 35.7 us
    pallas_call x1, Pallas kernels: 33.2 us -> 29.9 us  [exchange(): pl.pallas_call(functools.partial(exchange_kernel, slots), out_shape=[pltp...]
where the time goes in v5:
time: 36.3 us; the launch traced here: 36.2 us
  Pallas kernels  35.7 us (98%)
    pallas_call x1, Pallas kernels, exchange(): pl.pallas_call(functools.partial(exchange_kernel, slots), out_shape=[pltp...  29.9 us
    pallas_call x1, Pallas kernels, update(): pl.pallas_call(update_kernel, out_shape=[pltpu.HBM(matrix.shape, jnp.floa...  5.8 us

profile of v5, /device:TPU:0, one launch (start us, length us, event | category | flops | bytes accessed | tf_op | source)
XLA Modules:
  0.0 36.2 jit_solution(13843700675055332260)
XLA Ops:
  0.0 0.0 copy-start
  0.0 29.9 %exchange_24.1 = (f32[1024,2048]{1,0:T(8,128)S(1)}, f32[128,2048]{1,0:T(8,128)S(1)}, f32[1024,128]{1,0:T(8,128)S(1)}, f32[128,128]{1,0:T(8,128)S(1)}, f32[24,204...) custom-call(s32[1,128]{1,0:T(1,128)} %bitcast.4, f32[1024,2048]{1,0:T(8,128)} %matrix.1), custom_call_target="tpu_custom_call" | custom-call | tf_op jit(solution)/shard_map/exchange_24/pallas_call | solution.py:461
  29.9 0.0 copy-done
  30.0 6.0 %conditional.1 = (f32[1024,2048]{1,0:T(8,128)}) conditional(s32[]{:T(128)} %bitcast.1, (s32[1,128]{1,0:T(1,128)S(1)}, f32[1024,2048]{1,0:T(8,128)}) %tuple.17, (s32[2,128]{1,0:T(2,128)S(1)}, f32[1024,2048]{1,0:T(8,128)S(1)}, f32[128,2048]{1,0:T(8,128)S(1)}, f32[1024,128]{1,0:T(8,128)S(1)}, f32[128,128]{1,0:T(8,128)S(1)}, ...), branch_computations={%region_0.0_spmd, %region_1.0_spmd} | conditional | bytes 8 | solution.py:593
  30.0 5.8 %update.3 = (f32[1024,2048]{1,0:T(8,128)}, f32[1024,2048]{1,0:T(8,128)S(1)}) custom-call(s32[2,128]{1,0:T(2,128)S(1)} %get-tuple-element.33.note, f32[1024,2048]{1,0:T(8,128)S(1)} %get-tuple-element.34.block, f32[128,2048]{1,0:T(8,128)S(1)} %get-tuple-element.35.gathered, f32[1024,128]{1,0:T(8,128)S(1)} %get-tuple-element.36.panel, ...), custom_call_target="tpu_custom_call", output_to_operand_aliasing={{1}: (1, {})} | custom-call | tf_op jit(solution)/shard_map/cond/branch_1_fun/update/pallas_call | solution.py:564
Async XLA Ops:
  0.0 29.9 %copy-start = (s32[128]{0:T(128)S(1)}, s32[128]{0:T(128)}, u32[]{:S(2)}) copy-start(s32[128]{0:T(128)} %param.5) | copy-start | bytes 1540

commit v6 on v5

--- a/solution.py
+++ b/solution.py
@@ -14,14 +14,31 @@
 MIB = 1024 * 1024
 LOADS = 8
 WIDE = 256
-HIGHEST = lax.Precision.HIGHEST
+
+
+def split(value):
+    high = value.astype(jnp.bfloat16)
+    return high, (value - high.astype(jnp.float32)).astype(jnp.bfloat16)
+
+
+def stacked(value):
+    high, low = split(value)
+    return jnp.concatenate([high, low, high], axis=1)
+
+
+def terms(value):
+    high, low = split(value)
+    return jnp.concatenate([high, high, low], axis=0)
+
+
+def dot_parts(left, right):
+    return jnp.dot(stacked(left), terms(right), preferred_element_type=jnp.float32)
 
 
 def invert_unit_lower(block):
     rows = lax.broadcasted_iota(jnp.int32, (NB, NB), 0)
     cols = lax.broadcasted_iota(jnp.int32, (NB, NB), 1)
     eye = jnp.where(rows == cols, 1.0, 0.0).astype(jnp.float32)
-    dot = functools.partial(jnp.dot, precision=HIGHEST, preferred_element_type=jnp.float32)
     inverse = eye
     size = 1
     while size < NB:
@@ -30,7 +47,7 @@
         if size == 1:
             inverse = eye - part
         else:
-            inverse = inverse - dot(dot(inverse, part), inverse)
+            inverse = inverse - dot_parts(dot_parts(inverse, part), inverse)
         size *= 2
     return inverse
 
@@ -131,6 +148,23 @@
     other = jnp.where(core == 0, col + 1, col - 1)
     pivots_in = pltpu.make_async_copy(pivots_hbm, pivots, own_sem.at[10])
     pivots_in.start()
+    barrier = pltpu.get_barrier_semaphore()
+    for d in range(1, PROWS):
+        pl.semaphore_signal(barrier, inc=1, device_id={"prow": ahead(d)})
+    for c in (z_up, z_down, other):
+        pl.semaphore_signal(barrier, inc=1, device_id={"pcol": c})
+
+    @pl.when((me == 0) & (col == 0))
+    def _():
+        for c in (3, 4, 5, 7):
+            pl.semaphore_signal(barrier, inc=1, device_id={"pcol": c})
+
+    far = (col == 3) | (col == 4) | (col == 5) | (col == 7)
+
+    @pl.when((me == 0) & far)
+    def _():
+        pl.semaphore_signal(barrier, inc=1, device_id={"pcol": 0})
+
     panel_in = pltpu.make_async_copy(matrix.at[:, pl.ds(0, NB)], panel, own_sem.at[7])
 
     @pl.when(col == 0)
@@ -144,12 +178,8 @@
             pltpu.make_async_copy(matrix.at[part, :], resident.at[part, :], load_sem.at[k])
         )
         loads[-1].start()
-    barrier = pltpu.get_barrier_semaphore()
-    for d in range(1, PROWS):
-        pl.semaphore_signal(barrier, inc=1, device_id={"prow": ahead(d)})
-    for c in (z_up, z_down, other):
-        pl.semaphore_signal(barrier, inc=1, device_id={"pcol": c})
-    pl.semaphore_wait(barrier, PROWS - 1 + 3)
+    extra = jnp.where(me == 0, jnp.where(col == 0, 4, jnp.where(far, 1, 0)), 0)
+    pl.semaphore_wait(barrier, PROWS - 1 + 3 + extra)
 
     def top_x(d):
         return remote(
@@ -164,7 +194,37 @@
             top_send.at[0], top_recv.at[1], {"prow": d},
         )
 
-    loads[0].wait()
+    @pl.when(me == 0)
+    def _():
+        for c in loads[:1]:
+            c.wait()
+
+    def low_copy(k, device):
+        return remote(corner, corner, low_send.at[k], low_recv.at[0], device)
+
+    def low_sends_col(act):
+        @pl.when((me == 0) & (col == 0))
+        def _():
+            for c in (4, 5, 2, 6, 3, 7, 1):
+                act(low_copy(8 + c, {"pcol": c}))
+
+    def low_sends(act):
+        @pl.when(me == 0)
+        def _():
+            for d in (2, 1, 3):
+                act(low_copy(2 + d, {"prow": d * SIDE}))
+
+    def low_sends_y(act):
+        @pl.when(y == 0)
+        def _():
+            for d in (2, 1, 3):
+                act(low_copy(5 + d, {"prow": x * SIDE + d}))
+
+    @pl.when((me == 0) & (col == 0))
+    def _():
+        corner[...] = resident[pl.ds(0, NB), pl.ds(0, NB)]
+        low_sends_col(lambda c: c.start())
+        low_sends(lambda c: c.start())
 
     @pl.when(me == 0)
     def _():
@@ -176,38 +236,6 @@
         for k in range(SIDE):
             top_b[:, pl.ds(k * NB, NB)] = resident[pl.ds(half, half), pl.ds(k * SIDE * NB, NB)]
 
-    def low_copy(k, device):
-        return remote(corner, corner, low_send.at[k], low_recv.at[0], device)
-
-    def low_sends(act):
-        @pl.when(me == 0)
-        def _():
-            @pl.when(core == 0)
-            def _():
-                act(low_copy(0, {"pcol": other}))
-
-                @pl.when(z <= 1)
-                def _():
-                    act(low_copy(1, {"pcol": z_up}))
-
-                @pl.when(z == 0)
-                def _():
-                    act(low_copy(2, {"pcol": z_down}))
-
-            for d in (2, 1, 3):
-                act(low_copy(2 + d, {"prow": d * SIDE}))
-
-    def low_sends_y(act):
-        @pl.when(y == 0)
-        def _():
-            for d in (2, 1, 3):
-                act(low_copy(5 + d, {"prow": x * SIDE + d}))
-
-    @pl.when((me == 0) & (col == 0))
-    def _():
-        corner[...] = resident[pl.ds(0, NB), pl.ds(0, NB)]
-        low_sends(lambda c: c.start())
-
     def panel_copy(h, k, to):
         ref = panel.at[pl.ds(pl.multiple_of(h * (rows_dev // 2), 8), rows_dev // 2)]
         return remote(ref, ref, panel_send.at[k], panel_recv.at[h], {"pcol": to})
@@ -225,16 +253,22 @@
     plan_copy = pltpu.make_async_copy(table, plan, own_sem.at[9])
     plan_copy.start()
     plan_copy.wait()
+    @pl.when(me != 0)
+    def _():
+        for c in loads[:1]:
+            c.wait()
+
     for c in loads[1:]:
         c.wait()
 
-    def pick(s, carry):
-        row = resident[pl.ds(plan[1, s], 1), :]
-        for q in range(PROWS):
-            picks[pl.ds(q * slots + s, 1), :] = row[:, q * NB : (q + 1) * NB]
+    def pick(g, carry):
+        rows = [resident[pl.ds(plan[1, 2 * g + i], 1), :] for i in range(2)]
+        for i in range(2):
+            for q in range(PROWS):
+                picks[pl.ds(q * slots + 2 * g + i, 1), :] = rows[i][:, q * NB : (q + 1) * NB]
         return carry
 
-    lax.fori_loop(0, slots, pick, 0)
+    lax.fori_loop(0, slots // 2, pick, 0)
 
     def row_copy(d):
         peer = ahead(d)
@@ -273,10 +307,6 @@
         @pl.when(z == 0)
         def _():
             panel_copy(core, 1, z_down).start()
-
-    @pl.when((z != 2) & (col != 0))
-    def _():
-        panel_leg()
 
     def top_leg(a, d):
         if a == 0:
@@ -310,11 +340,13 @@
 
     row_all().wait_recv()
 
-    def order(j, carry):
-        ordered[pl.ds(j, 1), :] = received[pl.ds(plan[0, j], 1), :]
+    def order(g, carry):
+        rows = [received[pl.ds(plan[0, 16 * g + i], 1), :] for i in range(16)]
+        for i in range(16):
+            ordered[pl.ds(16 * g + i, 1), :] = rows[i]
         return carry
 
-    lax.fori_loop(0, NB, order, 0, unroll=8)
+    lax.fori_loop(0, NB // 16, order, 0)
     gathered[:, block(me)] = ordered[...]
 
     def spot(o, along, across):
@@ -344,6 +376,10 @@
         for o in (0, 1):
             ring_start(o, me, 0, spot(o, 0, d))
 
+    @pl.when((z != 2) & (col != 0))
+    def _():
+        panel_leg()
+
     @pl.when(y == 0)
     def _():
         @pl.when(x != 0)
@@ -360,13 +396,13 @@
     def _():
         top_leg(1, 1).wait_recv()
 
-    def back_rows(r, carry):
-        for s in range(slots):
-            index = plan[3, r * slots + s]
-            back[pl.ds(r * slots + s, 1), :] = top[pl.ds(index, 1), :]
+    def back_rows(g, carry):
+        rows = [top[pl.ds(plan[3, 16 * g + i], 1), :] for i in range(16)]
+        for i in range(16):
+            back[pl.ds(16 * g + i, 1), :] = rows[i]
         return carry
 
-    lax.fori_loop(0, PROWS, back_rows, 0)
+    lax.fori_loop(0, PROWS * slots // 16, back_rows, 0)
 
     def ret_copy(d):
         peer = ahead(d)
@@ -448,6 +484,7 @@
     def _():
         panel_copy(core, 1, other).wait_send()
 
+    low_sends_col(lambda c: c.wait_send())
     low_sends(lambda c: c.wait_send())
     low_sends_y(lambda c: c.wait_send())
 
@@ -485,7 +522,7 @@
             pltpu.VMEM((NB, NB), f32),
             dma((1,)), dma((1,)), dma((1,)), dma((1,)),
             dma((1,)), dma((7,)),
-            dma((3,)), dma((4,)), dma((4,)), dma((2,)), dma((10,)), dma((1,)), dma((11,)),
+            dma((3,)), dma((4,)), dma((4,)), dma((2,)), dma((16,)), dma((1,)), dma((11,)),
             dma((LOADS,)),
         ],
         compiler_params=pltpu.CompilerParams(
@@ -493,16 +530,6 @@
         ),
         name="exchange_%d" % slots,
     )(pivots, pltpu.with_memory_space_constraint(matrix, pltpu.HBM))
-
-
-def split(value):
-    high = value.astype(jnp.bfloat16)
-    return high, (value - high.astype(jnp.float32)).astype(jnp.bfloat16)
-
-
-def stacked(value):
-    high, low = split(value)
-    return jnp.concatenate([high, low, high], axis=1)
 
 
 def update_kernel(
@@ -527,10 +554,6 @@
         return pltpu.make_async_copy(
             result.at[:, pl.ds(n * WIDE, WIDE)], out.at[:, pl.ds(n * WIDE, WIDE)], sems.at[n]
         )
-
-    def terms(value):
-        high, low = split(value)
-        return jnp.concatenate([high, high, low], axis=0)
 
     rows = matrix.shape[0] - NB
     parts = matrix.shape[1] // WIDE

time: 36.3 us -> 35.5 us (0.978)
  no operation moved by 1% of the time
where the time goes in v6:
time: 35.5 us; the launch traced here: 35.4 us
  Pallas kernels  35.4 us (100%)
    pallas_call x1, Pallas kernels, exchange(): pl.pallas_call(functools.partial(exchange_kernel, slots), out_shape=[pltp...  29.7 us
    pallas_call x1, Pallas kernels, update(): pl.pallas_call(update_kernel, out_shape=[pltpu.HBM(matrix.shape, jnp.floa...  5.63 us

profile of v6, /device:TPU:0, one launch (start us, length us, event | category | flops | bytes accessed | tf_op | source)
XLA Modules:
  0.0 35.4 jit_solution(14957337906175984444)
XLA Ops:
  0.0 0.0 copy-start
  0.0 29.7 %exchange_24.1 = (f32[1024,2048]{1,0:T(8,128)S(1)}, f32[128,2048]{1,0:T(8,128)S(1)}, f32[1024,128]{1,0:T(8,128)S(1)}, f32[128,128]{1,0:T(8,128)S(1)}, f32[24,204...) custom-call(s32[1,128]{1,0:T(1,128)} %bitcast.4, f32[1024,2048]{1,0:T(8,128)} %matrix.1), custom_call_target="tpu_custom_call" | custom-call | tf_op jit(solution)/shard_map/exchange_24/pallas_call | solution.py:498
  29.8 0.0 copy-done
  29.8 5.6 %conditional.1 = (f32[1024,2048]{1,0:T(8,128)}) conditional(s32[]{:T(128)} %bitcast.1, (s32[1,128]{1,0:T(1,128)S(1)}, f32[1024,2048]{1,0:T(8,128)}) %tuple.17, (s32[2,128]{1,0:T(2,128)S(1)}, f32[1024,2048]{1,0:T(8,128)S(1)}, f32[128,2048]{1,0:T(8,128)S(1)}, f32[1024,128]{1,0:T(8,128)S(1)}, f32[128,128]{1,0:T(8,128)S(1)}, ...), branch_computations={%region_0.0_spmd, %region_1.0_spmd} | conditional | bytes 8 | solution.py:616
  29.8 5.6 %update.3 = (f32[1024,2048]{1,0:T(8,128)}, f32[1024,2048]{1,0:T(8,128)S(1)}) custom-call(s32[2,128]{1,0:T(2,128)S(1)} %get-tuple-element.33.note, f32[1024,2048]{1,0:T(8,128)S(1)} %get-tuple-element.34.block, f32[128,2048]{1,0:T(8,128)S(1)} %get-tuple-element.35.gathered, f32[1024,128]{1,0:T(8,128)S(1)} %get-tuple-element.36.panel, ...), custom_call_target="tpu_custom_call", output_to_operand_aliasing={{1}: (1, {})} | custom-call | tf_op jit(solution)/shard_map/cond/branch_1_fun/update/pallas_call | solution.py:587
Async XLA Ops:
  0.0 29.8 %copy-start = (s32[128]{0:T(128)S(1)}, s32[128]{0:T(128)}, u32[]{:S(2)}) copy-start(s32[128]{0:T(128)} %param.5) | copy-start | bytes 1540

commit v7 on v6

--- a/solution.py
+++ b/solution.py
@@ -12,7 +12,7 @@
 SIDE = 4
 FEW = 24
 MIB = 1024 * 1024
-LOADS = 8
+LOADS = 16
 WIDE = 256
 
 
@@ -196,7 +196,7 @@
 
     @pl.when(me == 0)
     def _():
-        for c in loads[:1]:
+        for c in loads[:2]:
             c.wait()
 
     def low_copy(k, device):
@@ -255,10 +255,10 @@
     plan_copy.wait()
     @pl.when(me != 0)
     def _():
-        for c in loads[:1]:
+        for c in loads[:2]:
             c.wait()
 
-    for c in loads[1:]:
+    for c in loads[2:]:
         c.wait()
 
     def pick(g, carry):

time: 35.5 us -> 35.6 us (level)
  no operation moved by 1% of the time
where the time goes in v7:
time: 35.6 us; the launch traced here: 35.5 us
  Pallas kernels  35.4 us (99%)
    pallas_call x1, Pallas kernels, exchange(): pl.pallas_call(functools.partial(exchange_kernel, slots), out_shape=[pltp...  29.8 us
    pallas_call x1, Pallas kernels, update(): pl.pallas_call(update_kernel, out_shape=[pltpu.HBM(matrix.shape, jnp.floa...  5.57 us

profile of v7, /device:TPU:0, one launch (start us, length us, event | category | flops | bytes accessed | tf_op | source)
XLA Modules:
  0.0 35.5 jit_solution(16688929505663335056)
XLA Ops:
  0.0 0.0 copy-start
  0.0 29.8 %exchange_24.1 = (f32[1024,2048]{1,0:T(8,128)S(1)}, f32[128,2048]{1,0:T(8,128)S(1)}, f32[1024,128]{1,0:T(8,128)S(1)}, f32[128,128]{1,0:T(8,128)S(1)}, f32[24,204...) custom-call(s32[1,128]{1,0:T(1,128)} %bitcast.4, f32[1024,2048]{1,0:T(8,128)} %matrix.1), custom_call_target="tpu_custom_call" | custom-call | tf_op jit(solution)/shard_map/exchange_24/pallas_call | solution.py:498
  29.9 0.0 copy-done
  29.9 5.6 %conditional.1 = (f32[1024,2048]{1,0:T(8,128)}) conditional(s32[]{:T(128)} %bitcast.1, (s32[1,128]{1,0:T(1,128)S(1)}, f32[1024,2048]{1,0:T(8,128)}) %tuple.17, (s32[2,128]{1,0:T(2,128)S(1)}, f32[1024,2048]{1,0:T(8,128)S(1)}, f32[128,2048]{1,0:T(8,128)S(1)}, f32[1024,128]{1,0:T(8,128)S(1)}, f32[128,128]{1,0:T(8,128)S(1)}, ...), branch_computations={%region_0.0_spmd, %region_1.0_spmd} | conditional | bytes 8 | solution.py:616
  29.9 5.6 %update.3 = (f32[1024,2048]{1,0:T(8,128)}, f32[1024,2048]{1,0:T(8,128)S(1)}) custom-call(s32[2,128]{1,0:T(2,128)S(1)} %get-tuple-element.33.note, f32[1024,2048]{1,0:T(8,128)S(1)} %get-tuple-element.34.block, f32[128,2048]{1,0:T(8,128)S(1)} %get-tuple-element.35.gathered, f32[1024,128]{1,0:T(8,128)S(1)} %get-tuple-element.36.panel, ...), custom_call_target="tpu_custom_call", output_to_operand_aliasing={{1}: (1, {})} | custom-call | tf_op jit(solution)/shard_map/cond/branch_1_fun/update/pallas_call | solution.py:587
Async XLA Ops:
  0.0 29.9 %copy-start = (s32[128]{0:T(128)S(1)}, s32[128]{0:T(128)}, u32[]{:S(2)}) copy-start(s32[128]{0:T(128)} %param.5) | copy-start | bytes 1540
